TPU v7x, 32 devices: a whole 2x2x4 slice. The times are simulated.
32 devices in a mesh: parts: 2 (over x), lon: 16 (over z, y, core).
Axes of the slice: x: 2, y: 2, z: 4, core: 2. Of those that a mesh axis runs over, the one named last changes fastest.
Arguments:
- carry_adjoint: float32 [32, 384, 2048], P('parts', 'lon'), parts along dimension 0, may hold values from -6 to 6
- east_courant: bfloat16 [32, 384, 2048], P('parts', 'lon'), parts along dimension 0, may hold values from -0.25 to 0.25
- north_courant: bfloat16 [32, 384, 2048], P('parts', 'lon'), parts along dimension 0, may hold values from -0.25 to 0.25
- sound_tile: int32 [32768, 1], P(('parts', 'lon')), parts along dimension 0, may hold values from 0 to 15; in each aligned block of 1024 rows (0 to 1023, 1024 to 2047, ...) at most 256 rows name the same one
- sound_cell: int32 [32768], P(('parts', 'lon')), parts along dimension 0, may hold values from 0 to 49151
- sound_kernel: float32 [32, 16384], P('parts', 'lon'), parts along dimension 0, may hold values from 0.2 to 1.5
- sound_weight: float32 [32768], P(('parts', 'lon')), parts along dimension 0, may hold values from -6 to 6
- cutoff: int32 [128], replicated, may hold values from 1 to 63, as said below
Outputs:
- initial_adjoint: float32 [32, 384, 2048], P('parts', 'lon'), parts along dimension 0
- flux_grad: float32 [768, 2048], P(('parts', 'lon')), parts along dimension 0
There are 2 independent parts, one for each index of `parts`. A program takes and returns all parts, laid end to end along the dimension named above; an argument that names none is the same for every part. Nothing has to cross between parts.
Inputs may be any that keep to these rules, and one draw needn't show every extreme that they name: `sound_tile`: among the soundings of one orbit segment (aligned blocks of 1024), at most 256 lie in the same tile. `cutoff`: entries 0 to 63 belong to the southern cap from the pole, the rest to the northern cap toward the pole.
All inputs are finite; a program needn't handle non-finite values.
Results may differ from a plain program's by a relative error of at most 0.0009.
Values may be sent and summed in bfloat16 or wider, within the bound.
A program may use at most 128 MiB of HBM per device.

v0:
```python
import math

import jax
import jax.numpy as jnp
from jax import lax
from jax.sharding import PartitionSpec as P

POLAR = 64
KMAX = 64


HIGH = lax.Precision.HIGHEST


def extended(x, sides, width):
    for axis, dim in sides:
        devices, length = (lax.axis_size(axis), x.shape[dim])
        up = [(i, (i + 1) % devices) for i in range(devices)]
        down = [(j, i) for i, j in up]
        last = lax.slice_in_dim(x, length - width, length, axis=dim)
        initial = lax.slice_in_dim(x, 0, width, axis=dim)
        before = lax.ppermute(last, axis, up)
        after = lax.ppermute(initial, axis, down)
        x = jnp.concatenate([before, x, after], axis=dim)
    return x


def shifted(block, axis, distance):
    devices = range(lax.axis_size(axis))
    route = [((i - distance) % len(devices), i) for i in devices]
    return lax.ppermute(block, axis, route)


def wave_table(longitudes, nlon):
    waves = jnp.arange(KMAX, dtype=jnp.int32)
    phase = longitudes[:, None] * waves[None, :] % nlon
    angle = phase.astype(jnp.float32) * (2.0 * math.pi / nlon)
    return jnp.concatenate([jnp.cos(angle), jnp.sin(angle)], axis=1)


def wave_scale(cut_rows, nlon):
    waves = jnp.arange(KMAX, dtype=jnp.int32)
    factor = jnp.where(waves == 0, 1.0, 2.0) / nlon
    kept = jnp.where(waves[None, :] <= cut_rows[:, None], factor[None, :], 0.0).astype(jnp.float32)
    return jnp.concatenate([kept, kept], axis=1)


def spectral(polar, cutoff):
    levels, width, caps = polar.shape
    lanes = lax.axis_size("lon")
    me = lax.axis_index("lon")
    nlon = width * lanes
    table = wave_table(me * width + jnp.arange(width, dtype=jnp.int32), nlon)
    partial_coef = jnp.einsum("lwr,wk->lrk", polar, table, precision=HIGH)
    total = lax.psum(partial_coef, "lon")
    scale = wave_scale(cutoff, nlon)
    return jnp.einsum("lrk,wk->lwr", total * scale[None], table, precision=HIGH)


def transport(padded, east, west, north, south):
    field = padded[:, 1:-1]
    right = padded[:, 2:]
    left = padded[:, :-2]
    column = jnp.zeros_like(field[:, :, :1])
    upper = jnp.concatenate([field[:, :, 1:], column], axis=2)
    lower = jnp.concatenate([column, field[:, :, :-1]], axis=2)
    out = field + jnp.maximum(east, 0) * (right - field) + jnp.minimum(west, 0) * (field - left)
    return out + jnp.maximum(north, 0) * (upper - field) + jnp.minimum(south, 0) * (field - lower)


def adjoint_step(field, cutoff, east, west, north, south):
    rows = field.shape[2]
    polar = jnp.concatenate([field[:, :, :POLAR], field[:, :, rows - POLAR :]], axis=2)
    smooth = spectral(polar, cutoff)
    filtered = jnp.concatenate(
        [smooth[:, :, :POLAR], field[:, :, POLAR : rows - POLAR], smooth[:, :, POLAR:]], axis=2
    )
    padded = extended(filtered, (("lon", 1),), 1)
    return transport(padded, east, west, north, south)


def per_device(
    carry_adjoint,
    east_courant,
    north_courant,
    sound_tile,
    sound_cell,
    sound_kernel,
    sound_weight,
    cutoff,
):
    levels, width, rows = carry_adjoint.shape
    lanes = lax.axis_size("lon")
    count = sound_weight.shape[0]
    slots = max(2, 4 * count // lanes)
    target = sound_tile[:, 0]
    onehot = (target[:, None] == jnp.arange(lanes, dtype=jnp.int32)[None, :]).astype(jnp.int32)
    rank = jnp.sum((jnp.cumsum(onehot, axis=0) - 1) * onehot, axis=1)
    position = target * slots + rank
    values = sound_kernel * sound_weight[None, :]
    outgoing = jnp.zeros((levels, lanes * slots), jnp.float32).at[:, position].set(values)
    places = jnp.zeros((lanes * slots,), jnp.int32).at[position].set(sound_cell)
    arrived, spots = (
        lax.all_to_all(
            outgoing.reshape(levels, lanes, slots).astype(jnp.bfloat16),
            "lon",
            split_axis=1,
            concat_axis=1,
            tiled=True,
        ).astype(jnp.float32),
        lax.all_to_all(
            places.reshape(1, lanes, slots), "lon", split_axis=1, concat_axis=1, tiled=True
        ),
    )
    forcing = (
        jnp.zeros((levels, width * rows), jnp.float32)
        .at[:, spots.reshape(-1)]
        .add(arrived.reshape(levels, -1))
    )
    final_adjoint = carry_adjoint + forcing.reshape(levels, width, rows)
    west_face = shifted(east_courant[:, width - 1 :, :], "lon", 1)
    west_courant = jnp.concatenate([west_face, east_courant[:, :-1, :]], axis=1)
    row_index = jnp.arange(rows, dtype=jnp.int32)
    north = jnp.where(
        row_index[None, None, :] < rows - 1, north_courant, jnp.zeros_like(north_courant)
    )
    south = jnp.concatenate([jnp.zeros_like(north[:, :, :1]), north[:, :, :-1]], axis=2)
    mid_adjoint = adjoint_step(final_adjoint, cutoff, east_courant, west_courant, north, south)
    initial_adjoint = adjoint_step(mid_adjoint, cutoff, east_courant, west_courant, north, south)
    flux_grad = final_adjoint[0] + mid_adjoint[0]
    return (initial_adjoint, flux_grad)


def solution(mesh):
    in_specs = (
        P("parts", "lon", None),
        P("parts", "lon", None),
        P("parts", "lon", None),
        P(("parts", "lon"), None),
        P(("parts", "lon")),
        P("parts", "lon"),
        P(("parts", "lon")),
        P(),
    )
    out_specs = (P("parts", "lon", None), P(("parts", "lon"), None))
    return jax.shard_map(
        per_device, mesh=mesh, in_specs=in_specs, out_specs=out_specs, check_vma=False
    )
```

profile of v0, /device:TPU:0, one launch (start us, length us, event | category | flops | bytes accessed | tf_op | source)
XLA Modules:
  0.0 343.7 jit_solution(12194055785980860410)
XLA Ops:
  7.2 0.7 fusion.31
  7.9 4.5 %reduce-window.6 = s32[16,8,128]{2,1,0:T(8,128)S(1)} reduce-window(s32[16,8,128]{2,1,0:T(8,128)S(1)} %fusion.31, s32[]{:T(128)} %constant.18.clone.1), window={size=1x1x128 pad=0_0x0_0x127_0}, to_apply=%region_0.0 | reduce-window | flops 2080768 | bytes 131076 | tf_op jit(solution)/shard_map/reduce-window
  12.4 0.1 slice.120
  12.4 0.1 copy.19
  12.6 0.1 copy.20
  12.7 0.1 add_add_fusion
  12.8 0.7 fusion.30
  13.5 0.7 compare_select_fusion.1
  14.2 5.1 %scatter_custom_fusion = s32[4096]{0:T(1024)} fusion(s32[1024]{0:T(1024)S(1)} %bitcast.58, s32[1024]{0:T(1024)} %param.12, s32[]{:T(128)} %constant.18.clone.1), kind=kCustom, calls=%fused_computation.75 | custom fusion | bytes 16896 | tf_op jit(solution)/shard_map/scatter | solution.py:102
  19.2 7.4 %all-to-all-start = ((s32[1,16,256]{2,0,1:T(1,128)}), s32[1,16,256]{2,0,1:T(1,128)S(1)}, u32[]{:S(2)}, u32[]{:S(2)}) async-start(s32[1,16,256]{2,0,1:T(1,128)} %bitcast.7), calls=%async_computation | async-start | bytes 32768 | tf_op jit(solution)/shard_map/all_to_all | solution.py:111
  26.6 1.8 slice.100
  28.5 0.4 collective-permute-start.1
  28.9 0.1 fusion.38
  29.0 0.7 fusion.32
  29.8 0.1 pad_maximum_fusion.4
  29.9 0.9 multiply_bitcast_fusion
  30.7 0.1 maximum_bitcast_fusion
  30.8 0.2 copy.21
  31.0 3.6 %scatter_custom_fusion.1 = f32[16,4096]{0,1:T(8,128)S(1)} fusion(s32[1024]{0:T(1024)S(1)} %bitcast.59, f32[1024,16]{1,0:T(8,128)S(1)} %copy.21, f32[]{:T(128)} %constant.20.clone.1), kind=kCustom, calls=%fused_computation.36 | custom fusion | bytes 262148 | tf_op jit(solution)/shard_map/scatter | solution.py:101
  34.6 0.1 convert_element_type.34
  34.7 1.0 copy.22
  35.7 0.0 all-to-all-done
  35.7 5.9 %all-to-all-start.1 = ((bf16[16,16,256]{2,0,1:T(8,128)(2,1)}), bf16[16,16,256]{2,0,1:T(8,128)(2,1)S(1)}, u32[]{:S(2)}, u32[]{:S(2)}) async-start(bf16[16,16,256]{2,0,1:T(8,128)(2,1)} %copy.22), calls=%async_computation.1 | async-start | bytes 262144 | tf_op jit(solution)/shard_map/all_to_all | solution.py:104
  41.6 0.0 all-reduce.8.cloned.1.call-start
  41.7 7.9 %all-to-all-done.1 = bf16[16,16,256]{2,0,1:T(8,128)(2,1)S(1)} async-done(((bf16[16,16,256]{2,0,1:T(8,128)(2,1)}), bf16[16,16,256]{2,0,1:T(8,128)(2,1)S(1)}, u32[]{:S(2)}, u32[]{:S(2)}) %all-to-all-start.1) | async-done | bytes 131104 | tf_op jit(solution)/shard_map/all_to_all | solution.py:104
  49.6 0.6 copy.24
  50.2 37.7 %scatter_custom_fusion.2 = f32[16,49152]{0,1:T(8,128)} fusion(s32[4096]{0:T(1024)S(1)} %bitcast.57, f32[4096,16]{1,0:T(8,128)S(1)} %copy.24, f32[]{:T(128)} %constant.20.clone.1), kind=kCustom, calls=%fused_computation.3 | custom fusion | flops 65536 | bytes 3145732 | tf_op jit(solution)/shard_map/scatter-add | solution.py:118
  87.9 16.0 %copy.26 = f32[16,24,2048]{2,1,0:T(8,128)} copy(f32[16,24,2048]{0,2,1:T(8,128)} %bitcast.44) | data formatting | bytes 6291456 | tf_op jit(solution)/shard_map/reshape | solution.py:120
  103.9 3.3 add.101
  107.3 0.1 fusion.50
  107.4 2.9 fusion.21
  110.3 0.0 all-reduce.8.cloned.1.call-update
  110.3 0.0 all-reduce.10.cloned.1.call-start
  110.3 2.7 broadcast_select_fusion
  113.0 2.4 slice.125
  115.4 85.9 %all-reduce.8.cloned.1.call-done = f32[16,128,128]{2,1,0:T(8,128)} async-done(((f32[16,128,128]{2,1,0:T(8,128)}), f32[16,128,128]{2,1,0:T(8,128)}) %all-reduce.8.cloned.1.call-update) | async-done | bytes 1048592 | tf_op jit(solution)/shard_map/psum | solution.py:55
  201.3 2.2 convolution_bitcast_fusion.1
  203.5 0.1 fusion.52
  203.6 3.6 %concatenate.55 = f32[16,24,2048]{2,1,0:T(8,128)S(1)} concatenate(f32[16,24,64]{2,1,0:T(8,128)S(1)} %get-tuple-element.17, f32[16,24,1920]{2,1,0:T(8,128)} %slice.125, f32[16,24,64]{2,1,0:T(8,128)S(1)} %get-tuple-element.16), dimensions={2} | concatenate | bytes 6291456 | tf_op jit(solution)/shard_map/concatenate | solution.py:75
  207.2 0.2 fusion.49
  207.4 1.2 collective-permute-start
  208.6 0.0 collective-permute-start.2
  208.6 1.3 fusion.48
  209.9 0.0 collective-permute-done.1
  209.9 1.2 collective-permute-done
  211.1 4.6 %collective-permute-done.2 = f32[16,1,2048]{2,1,0:T(1,128)S(1)} collective-permute-done((f32[16,1,2048]{2,1,0:T(1,128)S(1)}, f32[16,1,2048]{2,1,0:T(1,128)S(1)}, u32[]{:S(2)}, u32[]{:S(2)}) %collective-permute-start.2) | collective-permute-done | bytes 131104 | tf_op jit(solution)/shard_map/ppermute | solution.py:22
  215.7 5.1 %fusion.5 = f32[16,24,2048]{2,1,0:T(8,128)S(1)} fusion(f32[16,24,2048]{2,1,0:T(8,128)S(1)} %concatenate.55, f32[16,1,2048]{2,1,0:T(1,128)S(1)} %collective-permute-done.2, f32[16,1,2048]{2,1,0:T(1,128)S(1)} %collective-permute-done, f32[16,24,2047]{2,1,0:T(8,128)S(1)} %get-tuple-element.9, f32[16,24,2047]{2,1,0:T(8,128)S(1)} %get-tuple-element.8, ...), kind=kLoop, calls=%fused_computation.16 | loop fusion | flops 23592960 | bytes 19134720 | tf_op jit(solution)/shard_map/add | solution.py:68
  220.8 0.0 copy-start.2
  220.8 1.7 copy-done.2
  222.4 0.1 fusion.47
  222.5 2.9 fusion.25
  225.5 0.0 all-reduce.10.cloned.1.call-update
  225.5 4.4 %slice.135 = f32[16,24,1920]{2,1,0:T(8,128)} slice(f32[16,24,2048]{2,1,0:T(8,128)} %copy-done.2), slice={[0:16], [0:24], [64:1984]} | slice | bytes 5898240 | tf_op jit(solution)/shard_map/slice | solution.py:76
  229.9 1.7 fusion.20
  231.6 84.7 %all-reduce.10.cloned.1.call-done = f32[16,128,128]{2,1,0:T(8,128)} async-done(((f32[16,128,128]{2,1,0:T(8,128)}), f32[16,128,128]{2,1,0:T(8,128)}) %all-reduce.10.cloned.1.call-update) | async-done | bytes 1048592 | tf_op jit(solution)/shard_map/psum | solution.py:55
  316.2 2.2 convolution_bitcast_fusion
  318.4 0.1 fusion.51
  318.5 3.6 %concatenate.63 = f32[16,24,2048]{2,1,0:T(8,128)S(1)} concatenate(f32[16,24,64]{2,1,0:T(8,128)S(1)} %get-tuple-element.15, f32[16,24,1920]{2,1,0:T(8,128)} %slice.135, f32[16,24,64]{2,1,0:T(8,128)S(1)} %get-tuple-element.14), dimensions={2} | concatenate | bytes 6291456 | tf_op jit(solution)/shard_map/concatenate | solution.py:75
  322.1 0.2 fusion.46
  322.3 1.2 collective-permute-start.3
  323.5 1.3 fusion.45
  324.8 1.2 collective-permute-done.3
  326.0 4.6 %collective-permute-done.4 = f32[16,1,2048]{2,1,0:T(1,128)S(1)} collective-permute-done((f32[16,1,2048]{2,1,0:T(1,128)S(1)}, f32[16,1,2048]{2,1,0:T(1,128)S(1)}, u32[]{:S(2)}, u32[]{:S(2)}) %collective-permute-start.4) | collective-permute-done | bytes 131104 | tf_op jit(solution)/shard_map/ppermute | solution.py:22
  330.6 6.2 %fusion.9 = f32[16,24,2048]{2,1,0:T(8,128)} fusion(f32[16,24,2048]{2,1,0:T(8,128)S(1)} %concatenate.63, f32[16,1,2048]{2,1,0:T(1,128)S(1)} %collective-permute-done.4, f32[16,1,2048]{2,1,0:T(1,128)S(1)} %collective-permute-done.3, f32[16,24,2047]{2,1,0:T(8,128)S(1)} %get-tuple-element.3, f32[16,24,2047]{2,1,0:T(8,128)S(1)} %get-tuple-element.2, ...), kind=kLoop, calls=%fused_computation.20 | loop fusion | flops 23592960 | bytes 19134720 | tf_op jit(solution)/shard_map/add | solution.py:68
  (27 shorter events, 0.1 us)
Async XLA Ops:
  19.2 16.5 %all-to-all-start = ((s32[1,16,256]{2,0,1:T(1,128)}), s32[1,16,256]{2,0,1:T(1,128)S(1)}, u32[]{:S(2)}, u32[]{:S(2)}) async-start(s32[1,16,256]{2,0,1:T(1,128)} %bitcast.7), calls=%async_computation | async-start | bytes 32768 | tf_op jit(solution)/shard_map/all_to_all | solution.py:111
  28.5 181.4 %collective-permute-start.1 = (bf16[16,1,2048]{2,1,0:T(2,128)(2,1)}, bf16[16,1,2048]{2,1,0:T(2,128)(2,1)}, u32[]{:S(2)}, u32[]{:S(2)}) collective-permute-start(bf16[16,1,2048]{2,1,0:T(2,128)(2,1)} %slice.100), channel_id=1, source_target_pairs={{15,0},{0,1},{1,2},{2,3},{3,4},{4,5},{5,6},{6,7},{7,8},{8,9},{9,10... | collective-permute-start | bytes 196616 | tf_op jit(solution)/shard_map/ppermute | solution.py:31
  29.9 171.4 %copy-start.8 = (f32[128,128]{1,0:T(8,128)}, f32[128,128]{1,0:T(8,128)S(1)}, u32[]{:S(2)}) copy-start(f32[128,128]{1,0:T(8,128)S(1)} %pad_maximum_fusion.4) | copy-start | bytes 196612
  35.7 13.8 %all-to-all-start.1 = ((bf16[16,16,256]{2,0,1:T(8,128)(2,1)}), bf16[16,16,256]{2,0,1:T(8,128)(2,1)S(1)}, u32[]{:S(2)}, u32[]{:S(2)}) async-start(bf16[16,16,256]{2,0,1:T(8,128)(2,1)} %copy.22), calls=%async_computation.1 | async-start | bytes 262144 | tf_op jit(solution)/shard_map/all_to_all | solution.py:104
  41.6 159.7 %all-reduce.8.cloned.1.call-start = ((), (), s32[]{:S(2)}) async-start(), calls=%async_computation.2 | async-start | bytes 2097152 | tf_op jit(solution)/shard_map/psum | solution.py:55
  107.3 5.7 %copy-start.3 = (f32[16,24,2048]{2,1,0:T(8,128)}, f32[16,24,2048]{2,1,0:T(8,128)S(1)}, u32[]{:S(2)}) copy-start(f32[16,24,2048]{2,1,0:T(8,128)S(1)} %add.101) | copy-start | bytes 9437188
  110.3 206.0 %all-reduce.10.cloned.1.call-start = ((), (), s32[]{:S(2)}) async-start(), calls=%async_computation.3 | async-start | bytes 2097152 | tf_op jit(solution)/shard_map/psum | solution.py:55
  207.4 3.7 %collective-permute-start = (f32[16,1,2048]{2,1,0:T(1,128)S(1)}, f32[16,1,2048]{2,1,0:T(1,128)S(1)}, u32[]{:S(2)}, u32[]{:S(2)}) collective-permute-start(f32[16,1,2048]{2,1,0:T(1,128)S(1)} %get-tuple-element.10), channel_id=1, source_target_pairs={{1,0},{2,1},{3,2},{4,3},{5,4},{6,5},{7,6},{8,7},{9,8},{10,9},{11,1... | collective-permute-start | bytes 393224 | tf_op jit(solution)/shard_map/ppermute | solution.py:23
  208.6 7.1 %copy-start = (bf16[16,24,2048]{2,1,0:T(8,128)(2,1)S(1)}, bf16[16,24,2048]{2,1,0:T(8,128)(2,1)}, u32[]{:S(2)}) copy-start(bf16[16,24,2048]{2,1,0:T(8,128)(2,1)} %param.9) | copy-start | bytes 4718596
  208.6 7.1 %copy-start.4 = (bf16[16,24,2048]{2,1,0:T(8,128)(2,1)S(1)}, bf16[16,24,2048]{2,1,0:T(8,128)(2,1)}, u32[]{:S(2)}) copy-start(bf16[16,24,2048]{2,1,0:T(8,128)(2,1)} %param.10) | copy-start | bytes 4718596
  208.6 7.1 %copy-start.6 = (bf16[16,24,2048]{2,1,0:T(8,128)(2,1)S(1)}, bf16[16,24,2048]{2,1,0:T(8,128)(2,1)}, u32[]{:S(2)}) copy-start(bf16[16,24,2048]{2,1,0:T(8,128)(2,1)} %broadcast_select_fusion) | copy-start | bytes 4718596
  208.6 7.1 %collective-permute-start.2 = (f32[16,1,2048]{2,1,0:T(1,128)S(1)}, f32[16,1,2048]{2,1,0:T(1,128)S(1)}, u32[]{:S(2)}, u32[]{:S(2)}) collective-permute-start(f32[16,1,2048]{2,1,0:T(1,128)S(1)} %get-tuple-element.11), channel_id=1, source_target_pairs={{0,1},{1,2},{2,3},{3,4},{4,5},{5,6},{6,7},{7,8},{8,9},{9,10},{10,1... | collective-permute-start | bytes 393224 | tf_op jit(solution)/shard_map/ppermute | solution.py:22
  220.8 1.7 copy-start.2
  225.5 90.8 %copy-start.9 = (f32[128,128]{1,0:T(8,128)S(1)}, f32[128,128]{1,0:T(8,128)}, u32[]{:S(2)}) copy-start(f32[128,128]{1,0:T(8,128)} %copy-done.8) | copy-start | bytes 196612
  322.3 3.7 %collective-permute-start.3 = (f32[16,1,2048]{2,1,0:T(1,128)S(1)}, f32[16,1,2048]{2,1,0:T(1,128)S(1)}, u32[]{:S(2)}, u32[]{:S(2)}) collective-permute-start(f32[16,1,2048]{2,1,0:T(1,128)S(1)} %get-tuple-element.4), channel_id=1, source_target_pairs={{1,0},{2,1},{3,2},{4,3},{5,4},{6,5},{7,6},{8,7},{9,8},{10,9},{11,1... | collective-permute-start | bytes 393224 | tf_op jit(solution)/shard_map/ppermute | solution.py:23
  323.5 7.1 %copy-start.1 = (bf16[16,24,2048]{2,1,0:T(8,128)(2,1)S(1)}, bf16[16,24,2048]{2,1,0:T(8,128)(2,1)}, u32[]{:S(2)}) copy-start(bf16[16,24,2048]{2,1,0:T(8,128)(2,1)} %param.9) | copy-start | bytes 4718596
  323.5 7.1 %copy-start.5 = (bf16[16,24,2048]{2,1,0:T(8,128)(2,1)S(1)}, bf16[16,24,2048]{2,1,0:T(8,128)(2,1)}, u32[]{:S(2)}) copy-start(bf16[16,24,2048]{2,1,0:T(8,128)(2,1)} %param.10) | copy-start | bytes 4718596
  323.5 7.1 %copy-start.7 = (bf16[16,24,2048]{2,1,0:T(8,128)(2,1)S(1)}, bf16[16,24,2048]{2,1,0:T(8,128)(2,1)}, u32[]{:S(2)}) copy-start(bf16[16,24,2048]{2,1,0:T(8,128)(2,1)} %broadcast_select_fusion) | copy-start | bytes 4718596
  323.5 7.1 %collective-permute-start.4 = (f32[16,1,2048]{2,1,0:T(1,128)S(1)}, f32[16,1,2048]{2,1,0:T(1,128)S(1)}, u32[]{:S(2)}, u32[]{:S(2)}) collective-permute-start(f32[16,1,2048]{2,1,0:T(1,128)S(1)} %get-tuple-element.5), channel_id=1, source_target_pairs={{0,1},{1,2},{2,3},{3,4},{4,5},{5,6},{6,7},{7,8},{8,9},{9,10},{10,1... | collective-permute-start | bytes 393224 | tf_op jit(solution)/shard_map/ppermute | solution.py:22
Sparse Core Ops, SparseCore 0:
  110.4 90.8 all-reduce.7
  225.6 90.5 all-reduce.9
where the time goes:
time: 345 us; the launch traced here: 344 us
  waiting for transfers between devices  190 us (55%)
  other arithmetic  65.5 us (19%)
  local copies, waits for them, and re-layouts  47.6 us (14%)
  starting transfers between devices  16.1 us (5%)
  between operations  14.3 us (4%)
  matrix products  10.1 us (3%)
    psum x2, waiting for transfers between devices, spectral(): total = lax.psum(partial_coef, 'lon')  171 us
    scatter-add x1, other arithmetic, per_device(): forcing = jnp.zeros((levels, width * rows), jnp.float32).at[:, spots.resh...  37.7 us
    reshape x1, local copies, waits for them, and re-layouts, per_device(): final_adjoint = carry_adjoint + forcing.reshape(levels, width, rows)  16 us
    add x2, other arithmetic, transport(): out + jnp.maximum(north, 0) * (upper - field)  11.3 us
    ppermute x2, waiting for transfers between devices, extended(): before = lax.ppermute(last, axis, up)  9.15 us
    all_to_all x1, waiting for transfers between devices, per_device(): lax.all_to_all(outgoing.reshape(levels, lanes, slots).astype(jnp.bfloat16...  7.86 us
    all_to_all x1, starting transfers between devices, per_device(): lax.all_to_all(places.reshape(1, lanes, slots), 'lon', split_axis=1, conc...  7.39 us
    concatenate x2, local copies, waits for them, and re-layouts, adjoint_step(): jnp.concatenate([smooth[:, :, :POLAR], field[:, :, POLAR:rows - POLAR], s...  7.18 us
  transfers between devices with their start and end apart: 9, of which 7 were waited for; matrix products, arithmetic and copies ran while one was open for 26% of the time, Pallas kernels for 0%

commit v1 on v0

--- a/solution.py
+++ b/solution.py
@@ -1,15 +1,337 @@
+import functools
 import math
 
 import jax
 import jax.numpy as jnp
+import numpy as np
 from jax import lax
+from jax.experimental import pallas as pl
+from jax.experimental.pallas import tpu as pltpu
 from jax.sharding import PartitionSpec as P
 
 POLAR = 64
 KMAX = 64
-
+CAPS = 256
+KEEP = 66
+FIELDS = 32
 
 HIGH = lax.Precision.HIGHEST
+VMEM = pltpu.VMEM
+BF = jnp.bfloat16
+F32 = jnp.float32
+
+
+def nt_dot(a, b):
+    return lax.dot_general(a, b, (((1,), (1,)), ((), ())), preferred_element_type=F32)
+
+
+def route_kernel(lanes, slots, tile_ref, cell_ref, kernel_ref, weight_ref, east_ref, north_ref,
+                 message_ref, caps_ref, right_ref, left_ref):
+    levels, width, rows = east_ref.shape
+    count = tile_ref.shape[1]
+    tile = tile_ref[...]
+    cell = cell_ref[...]
+    member = lax.broadcasted_iota(jnp.int32, (lanes, count), 0) == tile
+    onehot = jnp.where(member, 1.0, 0.0)
+    before = lax.broadcasted_iota(jnp.int32, (count, count), 0) < lax.broadcasted_iota(
+        jnp.int32, (count, count), 1
+    )
+    earlier = jnp.dot(
+        onehot.astype(BF), jnp.where(before, 1.0, 0.0).astype(BF), preferred_element_type=F32
+    )
+    rank = jnp.sum(onehot * earlier, axis=0, keepdims=True).astype(jnp.int32)
+    place = lax.broadcasted_iota(jnp.int32, (slots, count), 0) == rank
+    place = jnp.where(place, 1.0, 0.0).astype(BF)
+    values = kernel_ref[...] * weight_ref[...]
+    lon = cell // rows
+    row = cell - lon * rows
+    high = row // 128
+    low = row - high * 128
+    index = lax.broadcasted_iota(jnp.int32, (FIELDS - levels, count), 0)
+    extra = jnp.where(index == 0, lon, jnp.where(index == 1, high, jnp.where(index == 2, low, 0)))
+    fields = jnp.concatenate([values, extra.astype(F32)], axis=0)
+    spread = [jnp.where(tile == d, fields, 0.0).astype(BF) for d in range(lanes)]
+    routed = nt_dot(jnp.concatenate(spread, axis=0), place)
+    message_ref[...] = routed.astype(BF).reshape(lanes, FIELDS, slots)
+    half = CAPS // 2
+    caps_ref[:, 0, :, :half] = east_ref[:, :, :half]
+    caps_ref[:, 0, :, half:] = east_ref[:, :, rows - half :]
+    caps_ref[:, 1, :, :half] = north_ref[:, :, :half]
+    caps_ref[:, 1, :, half:] = north_ref[:, :, rows - half :]
+    right_ref[0] = east_ref[:, width - 2, :]
+    right_ref[1] = east_ref[:, width - 1, :]
+    right_ref[2] = north_ref[:, width - 1, :]
+    left_ref[0] = east_ref[:, 0, :]
+    left_ref[1] = north_ref[:, 0, :]
+
+
+def scatter_kernel(arrived_ref, carry_ref, final_ref, right_ref, left_ref, spread_ref, row_ref):
+    levels, width, block = carry_ref.shape
+    sources, _, slots = arrived_ref.shape
+
+    @pl.when(pl.program_id(0) == 0)
+    def _():
+        for d in range(sources):
+            part = arrived_ref[d].astype(F32)
+            at = pl.ds(d * slots, slots)
+            lon = part[levels : levels + 1]
+            row_ref[:, at] = part[levels + 1 : levels + 2] * 128.0 + part[levels + 2 : levels + 3]
+            here = lax.broadcasted_iota(jnp.int32, (width, slots), 0).astype(F32) == lon
+            for l in range(levels):
+                spread_ref[l * width : (l + 1) * width, at] = jnp.where(
+                    here, part[l : l + 1], 0.0
+                ).astype(BF)
+
+    base = pl.program_id(0) * block
+    row_index = (lax.broadcasted_iota(jnp.int32, (block, sources * slots), 0) + base).astype(F32)
+    onehot = jnp.where(row_index == row_ref[...], 1.0, 0.0).astype(BF)
+    forcing = nt_dot(spread_ref[...], onehot)
+    final = carry_ref[...] + forcing.reshape(levels, width, block)
+    final_ref[...] = final
+    right_ref[0] = final[:, width - 2, :]
+    right_ref[1] = final[:, width - 1, :]
+    left_ref[0] = final[:, 0, :]
+    left_ref[1] = final[:, 1, :]
+
+
+def along_rows(field, north):
+    rows = field.shape[-1]
+    axis = field.ndim - 1
+    step = pltpu.roll(field, rows - 1, axis) - field
+    lower = pltpu.roll(jnp.minimum(north, 0.0) * step, 1, axis)
+    return jnp.maximum(north, 0.0) * step + lower
+
+
+def closed(north):
+    rows = north.shape[-1]
+    row = lax.broadcasted_iota(jnp.int32, north.shape, north.ndim - 1)
+    return jnp.where(row < rows - 1, north.astype(F32), 0.0)
+
+
+def polar_kernel(field_ref, courant_ref, cut_ref, table_ref, wide_ref, back_ref):
+    sources, width, lanes = field_ref.shape
+    nlon = sources * width
+    field = field_ref[...].astype(F32).reshape(nlon, lanes)
+    east = courant_ref[:, 0].astype(F32).reshape(nlon, lanes)
+    north = closed(courant_ref[:, 1].astype(F32).reshape(nlon, lanes))
+    wave = lax.broadcasted_iota(jnp.int32, (2 * KMAX, lanes), 0)
+    wave = jnp.where(wave >= KMAX, wave - KMAX, wave)
+    factor = jnp.where(wave == 0, 1.0 / nlon, 2.0 / nlon)
+    scale = jnp.where(wave <= cut_ref[...], factor, 0.0)
+    lane = lax.broadcasted_iota(jnp.int32, (nlon, lanes), 1)
+    polar = (lane < POLAR) | (lane >= lanes - POLAR)
+
+    def step(value):
+        coef = jnp.dot(wide_ref[...], value, precision=HIGH, preferred_element_type=F32)
+        smooth = jnp.dot(table_ref[...], coef * scale, precision=HIGH, preferred_element_type=F32)
+        value = jnp.where(polar, smooth, value)
+        change = pltpu.roll(value, nlon - 1, 0) - value
+        west = pltpu.roll(jnp.minimum(east, 0.0) * change, 1, 0)
+        return value + jnp.maximum(east, 0.0) * change + west + along_rows(value, north)
+
+    middle = step(field)
+    back_ref[:, 0] = step(middle).reshape(sources, width, lanes)
+    back_ref[:, 1] = (field + middle).reshape(sources, width, lanes)
+
+
+def band_kernel(final_ref, east_ref, north_ref, west_ref, right_ref, west_courant_ref,
+                right_courant_ref, own_ref, own_courant_ref, initial_ref, flux_ref, edge_ref):
+    levels, width, rows = final_ref.shape
+
+    def up(x):
+        return jnp.maximum(x, 0.0)
+
+    def down(x):
+        return jnp.minimum(x, 0.0)
+
+    @pl.when(pl.program_id(0) == 0)
+    def _():
+        near, far = west_ref[1], west_ref[0]
+        own_first, own_last = own_ref[0], own_ref[1]
+        change = own_first - near
+        e_near = west_courant_ref[1].astype(F32)
+        from_near = down(e_near) * change
+        before = near + up(e_near) * change + down(west_courant_ref[0].astype(F32)) * (near - far)
+        edge_ref[0] = from_near
+        edge_ref[1] = before + along_rows(near, closed(west_courant_ref[2]))
+        after, beyond = right_ref[0], right_ref[1]
+        e_after = right_courant_ref[0].astype(F32)
+        next_mid = after + up(e_after) * (beyond - after)
+        next_mid += down(own_courant_ref[...].astype(F32)) * (after - own_last)
+        edge_ref[2] = next_mid + along_rows(after, closed(right_courant_ref[1]))
+        edge_ref[3] = after
+        edge_ref[4] = down(e_near)
+
+    def level(l, _):
+        field = final_ref[l]
+        east = east_ref[l].astype(F32)
+        north = closed(north_ref[l])
+        at = lax.broadcasted_iota(jnp.int32, (width, rows), 0)
+        row = pl.ds(pl.program_id(0) * levels + l, 1)
+
+        def step(value, right, west):
+            right = jnp.where(at == width - 1, right, pltpu.roll(value, width - 1, 0))
+            change = right - value
+            west = jnp.where(at == 0, west, pltpu.roll(down(east) * change, 1, 0))
+            return value + up(east) * change + west + along_rows(value, north)
+
+        middle = step(field, edge_ref[3, row], edge_ref[0, row])
+        west = edge_ref[4, row] * (middle[0:1] - edge_ref[1, row])
+        initial_ref[l] = step(middle, edge_ref[2, row], west)
+
+        @pl.when((pl.program_id(0) == 0) & (l == 0))
+        def _():
+            flux_ref[...] = field + middle
+
+        return 0
+
+    lax.fori_loop(0, levels, level, 0)
+
+
+def merge_kernel(initial_ref, flux_ref, back_ref, flux_back_ref, initial_out, flux_out):
+    second = pl.program_id(0)
+    half = initial_ref.shape[-1]
+
+    def inside(shape):
+        lane = lax.broadcasted_iota(jnp.int32, shape, len(shape) - 1)
+        return jnp.where(second == 1, half - 1 - lane, lane) < KEEP
+
+    initial_out[...] = jnp.where(
+        inside(initial_ref.shape), back_ref[:, 0].astype(F32), initial_ref[...]
+    )
+    flux_out[...] = jnp.where(inside(flux_ref.shape), flux_back_ref[...].astype(F32), flux_ref[...])
+
+
+def full_table(nlon):
+    phase = np.arange(nlon)[:, None] * np.arange(KMAX)[None, :] % nlon
+    angle = phase * (2.0 * math.pi / nlon)
+    return np.concatenate([np.cos(angle), np.sin(angle)], axis=1).astype(np.float32)
+
+
+LIMIT = 48 * 1024 * 1024
+
+
+def params(**more):
+    return pltpu.CompilerParams(vmem_limit_bytes=LIMIT, **more)
+
+
+def cost(flops, moved):
+    return pl.CostEstimate(flops=flops, bytes_accessed=moved, transcendentals=0)
+
+
+def levels_spread(carry, east, north, sound_tile, sound_cell, sound_kernel, sound_weight, cutoff):
+    levels, width, rows = carry.shape
+    lanes = lax.axis_size("lon")
+    count = sound_weight.shape[0]
+    slots = max(2, 4 * count // lanes)
+    half = CAPS // 2
+    whole = pl.BlockSpec(memory_space=VMEM)
+    shape = jax.ShapeDtypeStruct
+    message, caps, to_right, to_left = pl.pallas_call(
+        functools.partial(route_kernel, lanes, slots),
+        out_shape=(
+            shape((lanes, FIELDS, slots), BF),
+            shape((levels, 2, width, CAPS), BF),
+            shape((3, levels, rows), BF),
+            shape((2, levels, rows), BF),
+        ),
+        in_specs=[whole] * 6,
+        out_specs=(whole,) * 4,
+        compiler_params=params(),
+        name="route",
+    )(
+        sound_tile.reshape(1, count),
+        sound_cell.reshape(1, count),
+        sound_kernel,
+        sound_weight.reshape(1, count),
+        east,
+        north,
+    )
+    arrived = lax.all_to_all(message, "lon", split_axis=0, concat_axis=0, tiled=True)
+    up = [(i, (i + 1) % lanes) for i in range(lanes)]
+    down = [(j, i) for i, j in up]
+    west_courant = lax.ppermute(to_right, "lon", up)
+    right_courant = lax.ppermute(to_left, "lon", down)
+    courant = lax.all_to_all(caps, "lon", split_axis=0, concat_axis=0, tiled=True)
+    block = 256
+    final, right_edge, left_edge = pl.pallas_call(
+        scatter_kernel,
+        grid=(rows // block,),
+        out_shape=(
+            shape((levels, width, rows), F32),
+            shape((2, levels, rows), F32),
+            shape((2, levels, rows), F32),
+        ),
+        in_specs=[
+            pl.BlockSpec((lanes, FIELDS, slots), lambda i: (0, 0, 0)),
+            pl.BlockSpec((levels, width, block), lambda i: (0, 0, i)),
+        ],
+        out_specs=(
+            pl.BlockSpec((levels, width, block), lambda i: (0, 0, i)),
+            pl.BlockSpec((2, levels, block), lambda i: (0, 0, i)),
+            pl.BlockSpec((2, levels, block), lambda i: (0, 0, i)),
+        ),
+        scratch_shapes=[
+            VMEM((levels * width, lanes * slots), BF),
+            VMEM((1, lanes * slots), F32),
+        ],
+        compiler_params=params(),
+        name="scatter",
+    )(arrived, carry)
+    polar = jnp.concatenate([final[:, :, :half], final[:, :, rows - half :]], axis=2)
+    gathered = lax.all_to_all(polar, "lon", split_axis=0, concat_axis=0, tiled=True)
+    west = lax.ppermute(right_edge, "lon", up)
+    right = lax.ppermute(left_edge, "lon", down)
+    own = jnp.stack([left_edge[0], right_edge[1]])
+    table = full_table(lanes * width)
+    spare = jnp.zeros((CAPS - 2 * POLAR,), jnp.int32)
+    cut = jnp.concatenate([cutoff[:POLAR], spare, cutoff[POLAR:]]).reshape(1, CAPS)
+    back = pl.pallas_call(
+        polar_kernel,
+        out_shape=shape((lanes, 2, width, CAPS), F32),
+        in_specs=[whole] * 5,
+        out_specs=whole,
+        compiler_params=params(),
+        name="polar",
+    )(gathered, courant, cut, jnp.asarray(table), jnp.asarray(table.T.copy()))
+    returned = lax.all_to_all(back, "lon", split_axis=0, concat_axis=0, tiled=True)
+    part = 4 if levels % 4 == 0 else levels
+    tile = pl.BlockSpec((part, width, rows), lambda i: (i, 0, 0))
+
+    def strip(n):
+        return pl.BlockSpec((n, levels, rows), lambda i: (0, 0, 0))
+
+    initial, flux = pl.pallas_call(
+        band_kernel,
+        grid=(levels // part,),
+        out_shape=(shape((levels, width, rows), F32), shape((width, rows), F32)),
+        in_specs=[tile, tile, tile, strip(2), strip(2), strip(3), strip(2), strip(2),
+                  pl.BlockSpec((levels, rows), lambda i: (0, 0))],
+        out_specs=(tile, pl.BlockSpec((width, rows), lambda i: (0, 0))),
+        scratch_shapes=[VMEM((5, levels, rows), F32)],
+        compiler_params=params(),
+        cost_estimate=cost(40 * levels * width * rows, 12 * levels * width * rows),
+        name="band",
+    )(final, east, north, west, right, west_courant, right_courant, own, to_right[1])
+    ends = rows // half - 1
+    return pl.pallas_call(
+        merge_kernel,
+        grid=(2,),
+        out_shape=(shape((levels, width, rows), F32), shape((width, rows), F32)),
+        in_specs=[
+            pl.BlockSpec((levels, width, half), lambda i: (0, 0, i * ends)),
+            pl.BlockSpec((width, half), lambda i: (0, i * ends)),
+            pl.BlockSpec((levels, 1, width, half), lambda i: (0, 0, 0, i)),
+            pl.BlockSpec((None, None, width, half), lambda i: (0, 1, 0, i)),
+        ],
+        out_specs=(
+            pl.BlockSpec((levels, width, half), lambda i: (0, 0, i * ends)),
+            pl.BlockSpec((width, half), lambda i: (0, i * ends)),
+        ),
+        input_output_aliases={0: 0, 1: 1},
+        compiler_params=params(),
+        name="merge",
+    )(initial, flux, returned, returned)
 
 
 def extended(x, sides, width):
@@ -79,7 +401,7 @@
     return transport(padded, east, west, north, south)
 
 
-def per_device(
+def any_lanes(
     carry_adjoint,
     east_courant,
     north_courant,
@@ -131,6 +453,12 @@
     return (initial_adjoint, flux_grad)
 
 
+def per_device(*arrays):
+    if arrays[0].shape[0] == lax.axis_size("lon"):
+        return levels_spread(*arrays)
+    return any_lanes(*arrays)
+
+
 def solution(mesh):
     in_specs = (
         P("parts", "lon", None),

time: 345 us -> 103 us (0.30)
  waiting for transfers between devices: 190 us -> 26.6 us
  other arithmetic: 65.5 us -> 0.86 us
  local copies, waits for them, and re-layouts: 47.6 us -> 8.84 us
  Pallas kernels: 0 us -> 26.2 us
  blocking collectives: 0 us -> 17.2 us
  between operations: 14.3 us -> 0.75 us
  matrix products: 10.1 us -> 0 us
  starting transfers between devices: 16.1 us -> 22.2 us
    psum x2 -> x0, waiting for transfers between devices: 171 us -> none  [spectral(): total = lax.psum(partial_coef, 'lon')]
    scatter-add x1 -> x0, other arithmetic: 37.7 us -> none  [per_device(): forcing = jnp.zeros((levels, width * rows), jnp.float32).at[:, spots.resh...]
    pallas_call x0 -> x5, Pallas kernels: none -> 26.2 us  [the longest x1 10.1 us: levels_spread(): pl.pallas_call(scatter_kernel, grid=(rows // block,), out_shape=(shape((l...]
    all_to_all x0 -> x1, blocking collectives: none -> 17.2 us  [levels_spread(): lax.all_to_all(message, 'lon', split_axis=0, concat_axis=0, tiled=True)]
    reshape x3 -> x0, local copies, waits for them, and re-layouts: 16.6 us -> none  [the longest x1 16 us: per_device(): final_adjoint = carry_adjoint + forcing.reshape(levels, width, rows)]
    add x5 -> x0, other arithmetic: 16.3 us -> none  [the longest x2 11.3 us: transport(): out + jnp.maximum(north, 0) * (upper - field)]
    slice x13 -> x4, local copies, waits for them, and re-layouts: 12.3 us -> 0.12 us  [the longest x1 0.07 us: levels_spread(): cutoff[:POLAR]]
    dot_general x4 -> x0, matrix products: 10.1 us -> none  [the longest x2 5.78 us: spectral(): partial_coef = jnp.einsum('lwr,wk->lrk', polar, table, precision=HIGH)]
  transfers between devices with their start and end apart: 9 -> 7, of which waited for: 7 -> 4; matrix products, arithmetic and copies ran while one was open for 26% -> 1% of each run, Pallas kernels for 0% -> 19%
where the time goes in v1:
time: 103 us
  waiting for transfers between devices  26.6 us (26%)
  Pallas kernels  26.2 us (25%)
  starting transfers between devices  22.2 us (22%)
  blocking collectives  17.2 us (17%)
  local copies, waits for them, and re-layouts  8.84 us (9%)
    all_to_all x1, blocking collectives, levels_spread(): lax.all_to_all(message, 'lon', split_axis=0, concat_axis=0, tiled=True)  17.2 us
    all_to_all x1, waiting for transfers between devices, levels_spread(): lax.all_to_all(polar, 'lon', split_axis=0, concat_axis=0, tiled=True)  12 us
    pallas_call x1, Pallas kernels, levels_spread(): pl.pallas_call(scatter_kernel, grid=(rows // block,), out_shape=(shape((l...  10.1 us
    pallas_call x1, Pallas kernels, levels_spread(): pl.pallas_call(band_kernel, grid=(levels // part,), out_shape=(shape((lev...  9.15 us
    unnamed x26, local copies, waits for them, and re-layouts  8.71 us
    ppermute x1, waiting for transfers between devices, levels_spread(): right_courant = lax.ppermute(to_left, 'lon', down)  6.15 us
    all_to_all x1, starting transfers between devices, levels_spread(): lax.all_to_all(polar, 'lon', split_axis=0, concat_axis=0, tiled=True)  5.97 us
    ppermute x1, waiting for transfers between devices, levels_spread(): west_courant = lax.ppermute(to_right, 'lon', up)  5.62 us
  transfers between devices with their start and end apart: 7, of which 4 were waited for; matrix products, arithmetic and copies ran while one was open for 1% of the time, Pallas kernels for 19%

profile of v1, /device:TPU:0, one launch (start us, length us, event | category | flops | bytes accessed | tf_op | source)
XLA Modules:
  0.0 102.7 jit_solution(13229076414909982907)
XLA Ops:
  0.6 0.0 copy-start
  0.6 1.4 %copy-done = bf16[16,24,2048]{2,1,0:T(8,128)(2,1)S(1)} copy-done((bf16[16,24,2048]{2,1,0:T(8,128)(2,1)S(1)}, bf16[16,24,2048]{2,1,0:T(8,128)(2,1)}, u32[]{:S(2)}) %copy-start) | copy-done | bytes 1572888
  2.0 0.0 copy-start.2
  2.0 1.4 %copy-done.2 = bf16[16,24,2048]{2,1,0:T(8,128)(2,1)S(1)} copy-done((bf16[16,24,2048]{2,1,0:T(8,128)(2,1)S(1)}, bf16[16,24,2048]{2,1,0:T(8,128)(2,1)}, u32[]{:S(2)}) %copy-start.2) | copy-done | bytes 1572888
  3.5 0.0 copy-start.7
  3.5 0.8 copy-done.7
  4.3 0.0 copy-start.8
  4.3 0.7 copy-done.8
  5.0 0.0 copy-start.9
  5.0 0.7 copy-done.9
  5.7 0.0 copy-start.10
  5.7 0.7 copy-done.10
  6.4 1.5 %route.1 = (bf16[16,32,256]{2,1,0:T(8,128)(2,1)S(1)}, bf16[16,2,24,256]{3,2,1,0:T(8,128)(2,1)}, bf16[3,16,2048]{2,1,0:T(8,128)(2,1)S(1)}, bf16[2,16,2048]{2,1,0:T(8,128)(2,1)S(1)}) custom-call(s32[1,1024]{1,0:T(1,128)S(1)} %bitcast.7, s32[1,1024]{1,0:T(1,128)S(1)} %bitcast.8, f32[16,1024]{1,0:T(8,128)S(1)} %copy-done.7, f32[1,1024]{1,0:T(1,128)S(1)} %bitcast.9, ...), custom_call_target="tpu_custom_call" | custom-call | tf_op jit(solution)/shard_map/route/pallas_call | solution.py:230
  7.8 0.0 copy-start.11
  7.8 17.2 %all_to_all.20.arrived_ref = bf16[16,32,256]{2,1,0:T(8,128)(2,1)S(1)} all-to-all(bf16[16,32,256]{2,1,0:T(8,128)(2,1)S(1)} %get-tuple-element.11), channel_id=1, replica_groups=mesh['parts'=2,'lon'=16] {'lon'}, dimensions={0} | all-to-all | bytes 524288 | tf_op jit(solution)/shard_map/all_to_all | solution.py:250
  25.1 0.0 copy-start.12
  25.1 0.0 copy-start.5
  25.1 0.0 copy-start.6
  25.1 3.7 %all-to-all-start.2 = ((bf16[16,2,24,256]{3,2,1,0:T(8,128)(2,1)}), bf16[16,2,24,256]{3,2,1,0:T(8,128)(2,1)S(1)}, u32[]{:S(2)}, u32[]{:S(2)}) async-start(bf16[16,2,24,256]{3,2,1,0:T(8,128)(2,1)} %get-tuple-element.19), calls=%async_computation.2 | async-start | bytes 786432 | tf_op jit(solution)/shard_map/all_to_all | solution.py:255
  28.8 10.1 %scatter.1 = (f32[16,24,2048]{2,1,0:T(8,128)S(1)}, f32[2,16,2048]{2,1,0:T(8,128)S(1)}, f32[2,16,2048]{2,1,0:T(8,128)S(1)}) custom-call(bf16[16,32,256]{2,1,0:T(8,128)(2,1)S(1)} %all_to_all.20.arrived_ref, f32[16,24,2048]{2,1,0:T(8,128)} %carry_ref.1), custom_call_target="tpu_custom_call" | custom-call | tf_op jit(solution)/shard_map/scatter/pallas_call | solution.py:257
  38.8 0.0 copy-start.4
  38.9 0.0 copy-done.11
  38.9 1.6 %copy-done.4 = f32[16,24,2048]{2,1,0:T(8,128)} copy-done((f32[16,24,2048]{2,1,0:T(8,128)}, f32[16,24,2048]{2,1,0:T(8,128)S(1)}, u32[]{:S(2)}) %copy-start.4) | copy-done | bytes 3145752
  40.5 0.0 copy-start.1
  40.5 0.8 pad_maximum_fusion
  41.2 0.0 all-to-all-done.2.courant_ref
  41.2 6.0 %all-to-all-start.1 = ((f32[16,24,256]{2,1,0:T(8,128)}), f32[16,24,256]{2,1,0:T(8,128)S(1)}, u32[]{:S(2)}, u32[]{:S(2)}) async-start(f32[16,24,256]{2,1,0:T(8,128)} %pad_maximum_fusion), calls=%async_computation.1 | async-start | bytes 786432 | tf_op jit(solution)/shard_map/all_to_all | solution.py:282
  47.2 0.0 copy-done.12
  47.2 0.1 fusion.1
  47.3 0.1 pad_add_fusion
  47.4 12.0 %all-to-all-done.1.field_ref = f32[16,24,256]{2,1,0:T(8,128)S(1)} async-done(((f32[16,24,256]{2,1,0:T(8,128)}), f32[16,24,256]{2,1,0:T(8,128)S(1)}, u32[]{:S(2)}, u32[]{:S(2)}) %all-to-all-start.1) | async-done | bytes 393248 | tf_op jit(solution)/shard_map/all_to_all | solution.py:282
  59.4 0.0 copy-done.5
  59.4 0.0 copy-done.6
  59.4 3.7 %polar.1 = f32[16,2,24,256]{3,2,1,0:T(8,128)} custom-call(f32[16,24,256]{2,1,0:T(8,128)S(1)} %all-to-all-done.1.field_ref, bf16[16,2,24,256]{3,2,1,0:T(8,128)(2,1)S(1)} %all-to-all-done.2.courant_ref, s32[1,256]{1,0:T(1,128)S(1)} %bitcast.6, f32[384,128]{1,0:T(8,128)S(1)} %copy-done.5, f32[128,384]{1,0:T(8,128)S(1)} %copy-done.6), custom_call_target="tpu_custom_call" | custom-call | tf_op jit(solution)/shard_map/polar/pallas_call | solution.py:289
  63.1 3.6 %all-to-all-start.3 = ((f32[16,2,24,256]{3,2,1,0:T(8,128)}), f32[16,2,24,256]{3,2,1,0:T(8,128)S(1)}, u32[]{:S(2)}, u32[]{:S(2)}) async-start(f32[16,2,24,256]{3,2,1,0:T(8,128)} %polar.1), calls=%async_computation.3 | async-start | bytes 1572864 | tf_op jit(solution)/shard_map/all_to_all | solution.py:297
  66.7 0.3 collective-permute-start.2
  67.1 4.2 %collective-permute-start.3 = (bf16[2,16,2048]{2,1,0:T(8,128)(2,1)}, bf16[2,16,2048]{2,1,0:T(8,128)(2,1)S(1)}, u32[]{:S(2)}, u32[]{:S(2)}) collective-permute-start(bf16[2,16,2048]{2,1,0:T(8,128)(2,1)} %copy-done.11), channel_id=1, source_target_pairs={{1,0},{2,1},{3,2},{4,3},{5,4},{6,5},{7,6},{8,7},{9,8},{10,9},{11,1... | collective-permute-start | bytes 393224 | tf_op jit(solution)/shard_map/ppermute | solution.py:254
  71.2 0.0 collective-permute-start
  71.2 4.4 %collective-permute-start.1 = (f32[2,16,2048]{2,1,0:T(8,128)S(1)}, f32[2,16,2048]{2,1,0:T(8,128)S(1)}, u32[]{:S(2)}, u32[]{:S(2)}) collective-permute-start(f32[2,16,2048]{2,1,0:T(8,128)S(1)} %get-tuple-element.14), channel_id=1, source_target_pairs={{1,0},{2,1},{3,2},{4,3},{5,4},{6,5},{7,6},{8,7},{9,8},{10,9},{11,1... | collective-permute-start | bytes 786440 | tf_op jit(solution)/shard_map/ppermute | solution.py:284
  75.7 6.1 %collective-permute-done.3.right_courant_ref = bf16[2,16,2048]{2,1,0:T(8,128)(2,1)S(1)} collective-permute-done((bf16[2,16,2048]{2,1,0:T(8,128)(2,1)}, bf16[2,16,2048]{2,1,0:T(8,128)(2,1)S(1)}, u32[]{:S(2)}, u32[]{:S(2)}) %collective-permute-start.3) | collective-permute-done | bytes 131104 | tf_op jit(solution)/shard_map/ppermute | solution.py:254
  81.9 5.6 %collective-permute-done.2.west_courant_ref = bf16[3,16,2048]{2,1,0:T(8,128)(2,1)S(1)} collective-permute-done((bf16[3,16,2048]{2,1,0:T(8,128)(2,1)S(1)}, bf16[3,16,2048]{2,1,0:T(8,128)(2,1)S(1)}, u32[]{:S(2)}, u32[]{:S(2)}) %collective-permute-start.2) | collective-permute-done | bytes 196640 | tf_op jit(solution)/shard_map/ppermute | solution.py:253
  87.5 2.8 %collective-permute-done.west_ref = f32[2,16,2048]{2,1,0:T(8,128)S(1)} collective-permute-done((f32[2,16,2048]{2,1,0:T(8,128)S(1)}, f32[2,16,2048]{2,1,0:T(8,128)S(1)}, u32[]{:S(2)}, u32[]{:S(2)}) %collective-permute-start) | collective-permute-done | bytes 262176 | tf_op jit(solution)/shard_map/ppermute | solution.py:283
  90.3 0.0 collective-permute-done.1.right_ref
  90.3 0.0 copy-done.1
  90.3 0.0 copy-start.3
  90.3 1.4 %copy-done.3 = bf16[16,24,2048]{2,1,0:T(8,128)(2,1)S(1)} copy-done((bf16[16,24,2048]{2,1,0:T(8,128)(2,1)S(1)}, bf16[16,24,2048]{2,1,0:T(8,128)(2,1)}, u32[]{:S(2)}) %copy-start.3) | copy-done | bytes 1572888
  91.7 9.1 %band.1 = (f32[16,24,2048]{2,1,0:T(8,128)}, f32[24,2048]{1,0:T(8,128)}) custom-call(f32[16,24,2048]{2,1,0:T(8,128)} %copy-done.4, bf16[16,24,2048]{2,1,0:T(8,128)(2,1)S(1)} %copy-done.1, bf16[16,24,2048]{2,1,0:T(8,128)(2,1)S(1)} %copy-done.3, f32[2,16,2048]{2,1,0:T(8,128)S(1)} %collective-permute-done.west_ref, ...), custom_call_target="tpu_custom_call" | custom-call | flops 31457280 | bytes 9437184 | tf_op jit(solution)/shard_map/band/pallas_call | solution.py:304
  100.9 0.0 all-to-all-done.3.back_ref.flux_back_ref
  100.9 1.8 %merge.1 = (f32[16,24,2048]{2,1,0:T(8,128)}, f32[24,2048]{1,0:T(8,128)}) custom-call(f32[16,24,2048]{2,1,0:T(8,128)} %get-tuple-element.17.initial_ref, f32[24,2048]{1,0:T(8,128)} %get-tuple-element.18.flux_ref, f32[16,2,24,256]{3,2,1,0:T(8,128)S(1)} %all-to-all-done.3.back_ref.flux_back_ref, ...), custom_call_target="tpu_custom_call", output_to_operand_aliasing={{0}: (0, {}), {1}: (1, {})} | custom-call | tf_op jit(solution)/shard_map/merge/pallas_call | solution.py:317
  (6 shorter events, 0.1 us)
Async XLA Ops:
  0.6 1.4 %copy-start = (bf16[16,24,2048]{2,1,0:T(8,128)(2,1)S(1)}, bf16[16,24,2048]{2,1,0:T(8,128)(2,1)}, u32[]{:S(2)}) copy-start(bf16[16,24,2048]{2,1,0:T(8,128)(2,1)} %east_ref.3) | copy-start | bytes 4718596
  2.0 1.4 %copy-start.2 = (bf16[16,24,2048]{2,1,0:T(8,128)(2,1)S(1)}, bf16[16,24,2048]{2,1,0:T(8,128)(2,1)}, u32[]{:S(2)}) copy-start(bf16[16,24,2048]{2,1,0:T(8,128)(2,1)} %north_ref.3) | copy-start | bytes 4718596
  3.5 0.8 copy-start.7
  4.3 0.7 copy-start.8
  5.0 0.7 copy-start.9
  5.7 0.7 copy-start.10
  7.8 31.0 %copy-start.11 = (bf16[2,16,2048]{2,1,0:T(8,128)(2,1)}, bf16[2,16,2048]{2,1,0:T(8,128)(2,1)S(1)}, u32[]{:S(2)}) copy-start(bf16[2,16,2048]{2,1,0:T(8,128)(2,1)S(1)} %get-tuple-element.16) | copy-start | bytes 393220
  25.1 22.2 %copy-start.12 = (s32[128]{0:T(128)S(1)}, s32[128]{0:T(128)}, u32[]{:S(2)}) copy-start(s32[128]{0:T(128)} %param.17) | copy-start | bytes 1540
  25.1 34.4 %copy-start.5 = (f32[384,128]{1,0:T(8,128)S(1)}, f32[384,128]{1,0:T(8,128)}, u32[]{:S(2)}) copy-start(f32[384,128]{1,0:T(8,128)} %constant.6.clone.table_ref) | copy-start | bytes 589828
  25.1 34.4 %copy-start.6 = (f32[128,384]{1,0:T(8,128)S(1)}, f32[128,384]{1,0:T(8,128)}, u32[]{:S(2)}) copy-start(f32[128,384]{1,0:T(8,128)} %constant.7.clone.wide_ref) | copy-start | bytes 589828
  25.1 16.2 %all-to-all-start.2 = ((bf16[16,2,24,256]{3,2,1,0:T(8,128)(2,1)}), bf16[16,2,24,256]{3,2,1,0:T(8,128)(2,1)S(1)}, u32[]{:S(2)}, u32[]{:S(2)}) async-start(bf16[16,2,24,256]{3,2,1,0:T(8,128)(2,1)} %get-tuple-element.19), calls=%async_computation.2 | async-start | bytes 786432 | tf_op jit(solution)/shard_map/all_to_all | solution.py:255
  38.8 1.6 %copy-start.4 = (f32[16,24,2048]{2,1,0:T(8,128)}, f32[16,24,2048]{2,1,0:T(8,128)S(1)}, u32[]{:S(2)}) copy-start(f32[16,24,2048]{2,1,0:T(8,128)S(1)} %get-tuple-element.12.final_ref) | copy-start | bytes 9437188
  40.5 49.9 %copy-start.1 = (bf16[16,24,2048]{2,1,0:T(8,128)(2,1)S(1)}, bf16[16,24,2048]{2,1,0:T(8,128)(2,1)}, u32[]{:S(2)}) copy-start(bf16[16,24,2048]{2,1,0:T(8,128)(2,1)} %east_ref.3) | copy-start | bytes 4718596
  41.2 18.2 %all-to-all-start.1 = ((f32[16,24,256]{2,1,0:T(8,128)}), f32[16,24,256]{2,1,0:T(8,128)S(1)}, u32[]{:S(2)}, u32[]{:S(2)}) async-start(f32[16,24,256]{2,1,0:T(8,128)} %pad_maximum_fusion), calls=%async_computation.1 | async-start | bytes 786432 | tf_op jit(solution)/shard_map/all_to_all | solution.py:282
  63.1 37.8 %all-to-all-start.3 = ((f32[16,2,24,256]{3,2,1,0:T(8,128)}), f32[16,2,24,256]{3,2,1,0:T(8,128)S(1)}, u32[]{:S(2)}, u32[]{:S(2)}) async-start(f32[16,2,24,256]{3,2,1,0:T(8,128)} %polar.1), calls=%async_computation.3 | async-start | bytes 1572864 | tf_op jit(solution)/shard_map/all_to_all | solution.py:297
  66.7 20.8 %collective-permute-start.2 = (bf16[3,16,2048]{2,1,0:T(8,128)(2,1)S(1)}, bf16[3,16,2048]{2,1,0:T(8,128)(2,1)S(1)}, u32[]{:S(2)}, u32[]{:S(2)}) collective-permute-start(bf16[3,16,2048]{2,1,0:T(8,128)(2,1)S(1)} %get-tuple-element.15), channel_id=1, source_target_pairs={{0,1},{1,2},{2,3},{3,4},{4,5},{5,6},{6,7},{7,8},{8,9},{9,10},{10,1... | collective-permute-start | bytes 589832 | tf_op jit(solution)/shard_map/ppermute | solution.py:253
  67.1 14.8 %collective-permute-start.3 = (bf16[2,16,2048]{2,1,0:T(8,128)(2,1)}, bf16[2,16,2048]{2,1,0:T(8,128)(2,1)S(1)}, u32[]{:S(2)}, u32[]{:S(2)}) collective-permute-start(bf16[2,16,2048]{2,1,0:T(8,128)(2,1)} %copy-done.11), channel_id=1, source_target_pairs={{1,0},{2,1},{3,2},{4,3},{5,4},{6,5},{7,6},{8,7},{9,8},{10,9},{11,1... | collective-permute-start | bytes 393224 | tf_op jit(solution)/shard_map/ppermute | solution.py:254
  71.2 19.1 %collective-permute-start = (f32[2,16,2048]{2,1,0:T(8,128)S(1)}, f32[2,16,2048]{2,1,0:T(8,128)S(1)}, u32[]{:S(2)}, u32[]{:S(2)}) collective-permute-start(f32[2,16,2048]{2,1,0:T(8,128)S(1)} %get-tuple-element.13), channel_id=1, source_target_pairs={{0,1},{1,2},{2,3},{3,4},{4,5},{5,6},{6,7},{7,8},{8,9},{9,10},{10,1... | collective-permute-start | bytes 786440 | tf_op jit(solution)/shard_map/ppermute | solution.py:283
  71.2 19.1 %collective-permute-start.1 = (f32[2,16,2048]{2,1,0:T(8,128)S(1)}, f32[2,16,2048]{2,1,0:T(8,128)S(1)}, u32[]{:S(2)}, u32[]{:S(2)}) collective-permute-start(f32[2,16,2048]{2,1,0:T(8,128)S(1)} %get-tuple-element.14), channel_id=1, source_target_pairs={{1,0},{2,1},{3,2},{4,3},{5,4},{6,5},{7,6},{8,7},{9,8},{10,9},{11,1... | collective-permute-start | bytes 786440 | tf_op jit(solution)/shard_map/ppermute | solution.py:284
  90.3 1.4 %copy-start.3 = (bf16[16,24,2048]{2,1,0:T(8,128)(2,1)S(1)}, bf16[16,24,2048]{2,1,0:T(8,128)(2,1)}, u32[]{:S(2)}) copy-start(bf16[16,24,2048]{2,1,0:T(8,128)(2,1)} %north_ref.3) | copy-start | bytes 4718596

commit v2 on v0

--- a/solution.py
+++ b/solution.py
@@ -1,15 +1,440 @@
+import functools
 import math
 
 import jax
 import jax.numpy as jnp
+import numpy as np
 from jax import lax
+from jax.experimental import pallas as pl
+from jax.experimental.pallas import tpu as pltpu
 from jax.sharding import PartitionSpec as P
 
 POLAR = 64
 KMAX = 64
-
+CAPS = 256
+KEEP = 66
+FIELDS = 32
 
 HIGH = lax.Precision.HIGHEST
+VMEM = pltpu.VMEM
+BF = jnp.bfloat16
+F32 = jnp.float32
+
+
+def nt_dot(a, b):
+    return lax.dot_general(a, b, (((1,), (1,)), ((), ())), preferred_element_type=F32)
+
+
+def along_rows(field, north):
+    rows = field.shape[-1]
+    axis = field.ndim - 1
+    step = pltpu.roll(field, rows - 1, axis) - field
+    lower = pltpu.roll(jnp.minimum(north, 0.0) * step, 1, axis)
+    return jnp.maximum(north, 0.0) * step + lower
+
+
+def closed(north):
+    rows = north.shape[-1]
+    row = lax.broadcasted_iota(jnp.int32, north.shape, north.ndim - 1)
+    return jnp.where(row < rows - 1, north.astype(F32), 0.0)
+
+
+class Exchange:
+    def __init__(self, lanes, send, receive, send_sem, receive_sem):
+        self.lanes, self.send, self.receive = lanes, send, receive
+        self.send_sem, self.receive_sem = send_sem, receive_sem
+        self.me = lax.axis_index("lon")
+
+    def copy(self, k, slot):
+        target = lax.rem(self.me + k, self.lanes)
+        return pltpu.make_async_remote_copy(
+            src_ref=self.send.at[target],
+            dst_ref=self.receive.at[slot],
+            send_sem=self.send_sem.at[k],
+            recv_sem=self.receive_sem.at[k],
+            device_id={"lon": target},
+            device_id_type=pl.DeviceIdType.MESH,
+        )
+
+    def start(self):
+        def one(k, _):
+            self.copy(k, self.me).start()
+            return 0
+
+        lax.fori_loop(1, self.lanes, one, 0)
+        self.receive[self.me] = self.send[self.me]
+
+    def arrive(self):
+        def one(k, _):
+            self.copy(k, lax.rem(self.me + self.lanes - k, self.lanes)).wait_recv()
+            return 0
+
+        lax.fori_loop(1, self.lanes, one, 0)
+
+    def leave(self):
+        def one(k, _):
+            self.copy(k, self.me).wait_send()
+            return 0
+
+        lax.fori_loop(1, self.lanes, one, 0)
+
+
+def window_kernel(tile_hbm, cell_hbm, kernel_hbm, weight_hbm, carry_hbm, east_hbm, north_hbm,
+                  cut_hbm, table_hbm, wide_hbm, initial_hbm, flux_hbm,
+                  tile_ref, cell_ref, kernel_ref, weight_ref, final_ref, east_ref, north_ref,
+                  cut_ref, table_ref, wide_ref, message, arrived, caps, courant, ends, circles,
+                  back, returned, flux_send, flux_caps, to_right, to_left, from_west, from_east,
+                  right_edge, left_edge, west_edge, east_edge, spread_ref, row_ref, edge_ref,
+                  initial_ref, flux_ref, load_sem, store_sem, all_send, all_receive, flux_sems,
+                  side_send, side_receive):
+    levels, width, rows = carry_hbm.shape
+    lanes, _, slots = message.shape
+    half = CAPS // 2
+    block = 256
+    me = lax.axis_index("lon")
+    right, left = lax.rem(me + 1, lanes), lax.rem(me + lanes - 1, lanes)
+    pairs = [(tile_hbm, tile_ref), (cell_hbm, cell_ref), (weight_hbm, weight_ref),
+             (kernel_hbm, kernel_ref), (east_hbm, east_ref), (north_hbm, north_ref),
+             (carry_hbm, final_ref), (cut_hbm, cut_ref), (table_hbm, table_ref),
+             (wide_hbm, wide_ref)]
+    loads = [pltpu.make_async_copy(a, b, load_sem.at[i]) for i, (a, b) in enumerate(pairs)]
+    for load in loads:
+        load.start()
+
+    barrier = pltpu.get_barrier_semaphore()
+
+    def greet(k, _):
+        pl.semaphore_signal(
+            barrier, inc=1, device_id={"lon": lax.rem(me + k, lanes)},
+            device_id_type=pl.DeviceIdType.MESH,
+        )
+        return 0
+
+    lax.fori_loop(1, lanes, greet, 0)
+
+    def side(send, receive, sem, target):
+        return pltpu.make_async_remote_copy(
+            src_ref=send, dst_ref=receive, send_sem=side_send.at[sem],
+            recv_sem=side_receive.at[sem], device_id={"lon": target},
+            device_id_type=pl.DeviceIdType.MESH,
+        )
+
+    for load in loads[:4]:
+        load.wait()
+    route(tile_ref, cell_ref, kernel_ref, weight_ref, message, rows)
+    pl.semaphore_wait(barrier, lanes - 1)
+    soundings = Exchange(lanes, message, arrived, all_send.at[0], all_receive.at[0])
+    soundings.start()
+
+    for load in loads[4:6]:
+        load.wait()
+    caps[:, 0, :, :half] = east_ref[:, :, :half]
+    caps[:, 0, :, half:] = east_ref[:, :, rows - half :]
+    caps[:, 1, :, :half] = north_ref[:, :, :half]
+    caps[:, 1, :, half:] = north_ref[:, :, rows - half :]
+    winds = Exchange(lanes, caps, courant, all_send.at[1], all_receive.at[1])
+    winds.start()
+    to_right[0] = east_ref[:, width - 2, :]
+    to_right[1] = east_ref[:, width - 1, :]
+    to_right[2] = north_ref[:, width - 1, :]
+    to_left[0] = east_ref[:, 0, :]
+    to_left[1] = north_ref[:, 0, :]
+    wind_sides = [side(to_right, from_west, 0, right), side(to_left, from_east, 1, left)]
+    for copy in wind_sides:
+        copy.start()
+
+    soundings.arrive()
+    for d in range(lanes):
+        part = arrived[d]
+        at = pl.ds(d * slots, slots)
+        wide = part[levels : levels + 8].astype(F32)
+        row_ref[:, at] = wide[1:2] * 128.0 + wide[2:3]
+        here = lax.broadcasted_iota(jnp.int32, (width, slots), 0).astype(F32) == wide[0:1]
+        values = part[:levels].astype(F32)
+        for l in range(levels):
+            spread_ref[l * width : (l + 1) * width, at] = jnp.where(
+                here, values[l : l + 1], 0.0
+            ).astype(BF)
+    loads[6].wait()
+
+    def scatter(base):
+        at = pl.ds(base, block)
+        row = row_ref[...] - jnp.asarray(base, F32)
+        row = jnp.where((row >= 0) & (row < block), row, -1.0).astype(BF)
+        index = lax.broadcasted_iota(jnp.int32, (block, lanes * slots), 0).astype(F32).astype(BF)
+        onehot = jnp.where(index == row, jnp.ones((), BF), jnp.zeros((), BF))
+        forcing = nt_dot(spread_ref[...], onehot)
+        final_ref[:, :, at] = final_ref[:, :, at] + forcing.reshape(levels, width, block)
+
+    scatter(0)
+    scatter(rows - block)
+    ends[:, :, :half] = final_ref[:, :, :half]
+    ends[:, :, half:] = final_ref[:, :, rows - half :]
+    polar = Exchange(lanes, ends, circles, all_send.at[2], all_receive.at[2])
+    polar.start()
+
+    def middle_block(i, _):
+        scatter(pl.multiple_of(i * block, block))
+        return 0
+
+    lax.fori_loop(1, rows // block - 1, middle_block, 0)
+    right_edge[0] = final_ref[:, width - 2, :]
+    right_edge[1] = final_ref[:, width - 1, :]
+    left_edge[0] = final_ref[:, 0, :]
+    left_edge[1] = final_ref[:, 1, :]
+    field_sides = [side(right_edge, west_edge, 2, right), side(left_edge, east_edge, 3, left)]
+    for copy in field_sides:
+        copy.start()
+
+    for load in loads[7:]:
+        load.wait()
+    winds.arrive()
+    polar.arrive()
+    polar_steps(circles, courant, cut_ref, table_ref, wide_ref, back, flux_send)
+    answer = Exchange(lanes, back, returned, all_send.at[3], all_receive.at[3])
+    answer.start()
+
+    def flux_copy(k):
+        return pltpu.make_async_remote_copy(
+            src_ref=flux_send.at[k], dst_ref=flux_caps, send_sem=flux_sems.at[k],
+            recv_sem=flux_sems.at[0], device_id={"lon": k},
+            device_id_type=pl.DeviceIdType.MESH,
+        )
+
+    @pl.when(me == 0)
+    def _():
+        def one(k, _):
+            flux_copy(k).start()
+            return 0
+
+        lax.fori_loop(1, lanes, one, 0)
+        flux_caps[...] = flux_send[0]
+
+    for copy in wind_sides + field_sides:
+        copy.wait_recv()
+    side_edges(west_edge, east_edge, from_west, from_east, left_edge, right_edge, to_right, edge_ref)
+
+    inner = pl.ds(half, rows - CAPS)
+
+    def store(l):
+        return pltpu.make_async_copy(
+            initial_ref.at[l, :, inner], initial_hbm.at[l, :, inner], store_sem.at[l]
+        )
+
+    def level(l, _):
+        middle = band(l, final_ref, east_ref, north_ref, edge_ref, initial_ref)
+        store(l).start()
+
+        @pl.when(l == 0)
+        def _():
+            flux_ref[...] = final_ref[0] + middle
+
+        return 0
+
+    lax.fori_loop(0, levels, level, 0)
+    answer.arrive()
+
+    @pl.when(me != 0)
+    def _():
+        flux_copy(1).wait_recv()
+
+    lane = lax.broadcasted_iota(jnp.int32, (width, half), 1)
+    lasts = []
+    for i, at in enumerate((pl.ds(0, half), pl.ds(rows - half, half))):
+        inside = (lane if i == 0 else half - 1 - lane) < KEEP
+        side_at = pl.ds(i * half, half)
+        for l in range(levels):
+            initial_ref[l, :, at] = jnp.where(inside, returned[l, :, side_at], initial_ref[l, :, at])
+        flux_ref[:, at] = jnp.where(inside, flux_caps[:, side_at], flux_ref[:, at])
+        lasts.append(pltpu.make_async_copy(
+            initial_ref.at[:, :, at], initial_hbm.at[:, :, at], store_sem.at[levels + i]
+        ))
+        lasts[-1].start()
+    lasts.append(pltpu.make_async_copy(flux_ref, flux_hbm, store_sem.at[levels + 2]))
+    lasts[-1].start()
+
+    for copy in wind_sides + field_sides:
+        copy.wait_send()
+    for exchange in (soundings, winds, polar, answer):
+        exchange.leave()
+
+    @pl.when(me == 0)
+    def _():
+        def one(k, _):
+            flux_copy(k).wait_send()
+            return 0
+
+        lax.fori_loop(1, lanes, one, 0)
+
+    def stored(l, _):
+        store(l).wait()
+        return 0
+
+    lax.fori_loop(0, levels, stored, 0)
+    for copy in lasts:
+        copy.wait()
+
+
+def route(tile_ref, cell_ref, kernel_ref, weight_ref, message, rows):
+    lanes, _, slots = message.shape
+    levels, count = kernel_ref.shape
+    tile = tile_ref[...]
+    cell = cell_ref[...]
+    member = lax.broadcasted_iota(jnp.int32, (lanes, count), 0) == tile
+    onehot = jnp.where(member, 1.0, 0.0)
+    before = lax.broadcasted_iota(jnp.int32, (count, count), 0) < lax.broadcasted_iota(
+        jnp.int32, (count, count), 1
+    )
+    earlier = jnp.dot(
+        onehot.astype(BF), jnp.where(before, 1.0, 0.0).astype(BF), preferred_element_type=F32
+    )
+    rank = jnp.sum(onehot * earlier, axis=0, keepdims=True).astype(jnp.int32)
+    place = lax.broadcasted_iota(jnp.int32, (slots, count), 0) == rank
+    place = jnp.where(place, 1.0, 0.0).astype(BF)
+    values = kernel_ref[...] * weight_ref[...]
+    lon = cell // rows
+    row = cell - lon * rows
+    high = row // 128
+    low = row - high * 128
+    index = lax.broadcasted_iota(jnp.int32, (FIELDS - levels, count), 0)
+    extra = jnp.where(index == 0, lon, jnp.where(index == 1, high, jnp.where(index == 2, low, 0)))
+    fields = jnp.concatenate([values, extra.astype(F32)], axis=0)
+    spread = [jnp.where(tile == d, fields, 0.0).astype(BF) for d in range(lanes)]
+    routed = nt_dot(jnp.concatenate(spread, axis=0), place)
+    message[...] = routed.astype(BF).reshape(lanes, FIELDS, slots)
+
+
+def polar_steps(field_ref, courant_ref, cut_ref, table_ref, wide_ref, back_ref, flux_send):
+    sources, width, lanes = field_ref.shape
+    nlon = sources * width
+    field = field_ref[...].reshape(nlon, lanes)
+    east = courant_ref[:, 0].astype(F32).reshape(nlon, lanes)
+    north = closed(courant_ref[:, 1].astype(F32).reshape(nlon, lanes))
+    wave = lax.broadcasted_iota(jnp.int32, (2 * KMAX, lanes), 0)
+    wave = jnp.where(wave >= KMAX, wave - KMAX, wave)
+    factor = jnp.where(wave == 0, 1.0 / nlon, 2.0 / nlon)
+    scale = jnp.where(wave <= cut_ref[...], factor, 0.0)
+    lane = lax.broadcasted_iota(jnp.int32, (nlon, lanes), 1)
+    polar = (lane < POLAR) | (lane >= lanes - POLAR)
+
+    def step(value):
+        coef = jnp.dot(wide_ref[...], value, precision=HIGH, preferred_element_type=F32)
+        smooth = jnp.dot(table_ref[...], coef * scale, precision=HIGH, preferred_element_type=F32)
+        value = jnp.where(polar, smooth, value)
+        change = pltpu.roll(value, nlon - 1, 0) - value
+        west = pltpu.roll(jnp.minimum(east, 0.0) * change, 1, 0)
+        return value + jnp.maximum(east, 0.0) * change + west + along_rows(value, north)
+
+    middle = step(field)
+    flux_send[...] = (field + middle).reshape(sources, width, lanes)
+    back_ref[...] = step(middle).reshape(sources, width, lanes)
+
+
+def up(x):
+    return jnp.maximum(x, 0.0)
+
+
+def down(x):
+    return jnp.minimum(x, 0.0)
+
+
+def side_edges(west_ref, right_ref, west_courant_ref, right_courant_ref, left_edge, right_edge,
+               to_right, edge_ref):
+    near, far = west_ref[1], west_ref[0]
+    own_first, own_last = left_edge[0], right_edge[1]
+    change = own_first - near
+    e_near = west_courant_ref[1].astype(F32)
+    from_near = down(e_near) * change
+    before = near + up(e_near) * change + down(west_courant_ref[0].astype(F32)) * (near - far)
+    edge_ref[0] = from_near
+    edge_ref[1] = before + along_rows(near, closed(west_courant_ref[2]))
+    after, beyond = right_ref[0], right_ref[1]
+    e_after = right_courant_ref[0].astype(F32)
+    next_mid = after + up(e_after) * (beyond - after)
+    next_mid += down(to_right[1].astype(F32)) * (after - own_last)
+    edge_ref[2] = next_mid + along_rows(after, closed(right_courant_ref[1]))
+    edge_ref[3] = after
+    edge_ref[4] = down(e_near)
+
+
+def band(l, final_ref, east_ref, north_ref, edge_ref, initial_ref):
+    levels, width, rows = final_ref.shape
+    row = pl.ds(l, 1)
+    field = final_ref[l]
+    east = east_ref[l].astype(F32)
+    north = closed(north_ref[l])
+    at = lax.broadcasted_iota(jnp.int32, (width, rows), 0)
+
+    def step(value, right, west):
+        right = jnp.where(at == width - 1, right, pltpu.roll(value, width - 1, 0))
+        change = right - value
+        west = jnp.where(at == 0, west, pltpu.roll(down(east) * change, 1, 0))
+        return value + up(east) * change + west + along_rows(value, north)
+
+    middle = step(field, edge_ref[3, row], edge_ref[0, row])
+    west = edge_ref[4, row] * (middle[0:1] - edge_ref[1, row])
+    initial_ref[l] = step(middle, edge_ref[2, row], west)
+    return middle
+
+
+def full_table(nlon):
+    phase = np.arange(nlon)[:, None] * np.arange(KMAX)[None, :] % nlon
+    angle = phase * (2.0 * math.pi / nlon)
+    return np.concatenate([np.cos(angle), np.sin(angle)], axis=1).astype(np.float32)
+
+
+LIMIT = 56 * 1024 * 1024
+
+
+def levels_spread(carry, east, north, sound_tile, sound_cell, sound_kernel, sound_weight, cutoff):
+    levels, width, rows = carry.shape
+    lanes = lax.axis_size("lon")
+    nlon = lanes * width
+    count = sound_weight.shape[0]
+    slots = max(2, 4 * count // lanes)
+    shape = jax.ShapeDtypeStruct
+    table = full_table(nlon)
+    spare = jnp.zeros((CAPS - 2 * POLAR,), jnp.int32)
+    cut = jnp.concatenate([cutoff[:POLAR], spare, cutoff[POLAR:]]).reshape(1, CAPS)
+    anywhere = pl.BlockSpec(memory_space=pl.ANY)
+    return pl.pallas_call(
+        window_kernel,
+        out_shape=(shape((levels, width, rows), F32), shape((width, rows), F32)),
+        in_specs=[anywhere] * 10,
+        out_specs=(anywhere,) * 2,
+        scratch_shapes=[
+            VMEM((1, count), jnp.int32), VMEM((1, count), jnp.int32),
+            VMEM((levels, count), F32), VMEM((1, count), F32),
+            VMEM((levels, width, rows), F32),
+            VMEM((levels, width, rows), BF), VMEM((levels, width, rows), BF),
+            VMEM((1, CAPS), jnp.int32),
+            VMEM((nlon, 2 * KMAX), F32), VMEM((2 * KMAX, nlon), F32),
+            VMEM((lanes, FIELDS, slots), BF), VMEM((lanes, FIELDS, slots), BF),
+            VMEM((lanes, 2, width, CAPS), BF), VMEM((lanes, 2, width, CAPS), BF),
+            VMEM((lanes, width, CAPS), F32), VMEM((lanes, width, CAPS), F32),
+            VMEM((lanes, width, CAPS), F32), VMEM((lanes, width, CAPS), F32),
+            VMEM((lanes, width, CAPS), F32), VMEM((width, CAPS), F32),
+            VMEM((3, levels, rows), BF), VMEM((2, levels, rows), BF),
+            VMEM((3, levels, rows), BF), VMEM((2, levels, rows), BF),
+            VMEM((2, levels, rows), F32), VMEM((2, levels, rows), F32),
+            VMEM((2, levels, rows), F32), VMEM((2, levels, rows), F32),
+            VMEM((levels * width, lanes * slots), BF), VMEM((1, lanes * slots), F32),
+            VMEM((5, levels, rows), F32),
+            VMEM((levels, width, rows), F32), VMEM((width, rows), F32),
+            pltpu.SemaphoreType.DMA((10,)), pltpu.SemaphoreType.DMA((levels + 3,)),
+            pltpu.SemaphoreType.DMA((4, lanes)), pltpu.SemaphoreType.DMA((4, lanes)),
+            pltpu.SemaphoreType.DMA((lanes,)),
+            pltpu.SemaphoreType.DMA((4,)), pltpu.SemaphoreType.DMA((4,)),
+        ],
+        compiler_params=pltpu.CompilerParams(
+            vmem_limit_bytes=LIMIT, collective_id=0, has_side_effects=True
+        ),
+        name="window",
+    )(
+        sound_tile.reshape(1, count), sound_cell.reshape(1, count), sound_kernel,
+        sound_weight.reshape(1, count), carry, east, north, cut, jnp.asarray(table),
+        jnp.asarray(table.T.copy()),
+    )
 
 
 def extended(x, sides, width):
@@ -79,7 +504,7 @@
     return transport(padded, east, west, north, south)
 
 
-def per_device(
+def any_lanes(
     carry_adjoint,
     east_courant,
     north_courant,
@@ -131,6 +556,12 @@
     return (initial_adjoint, flux_grad)
 
 
+def per_device(*arrays):
+    if arrays[0].shape[0] == lax.axis_size("lon"):
+        return levels_spread(*arrays)
+    return any_lanes(*arrays)
+
+
 def solution(mesh):
     in_specs = (
         P("parts", "lon", None),

time: 345 us -> 56 us (0.16)
  the two profiles are of different devices: /device:TPU:0 before, /device:TPU:29 now
where the time goes in v2:
time: 56 us; the launch traced here: 55.8 us
  Pallas kernels  49.1 us (88%)
  local copies, waits for them, and re-layouts  5.43 us (10%)
  between operations  0.65 us (1%)
  other arithmetic  0.64 us (1%)
    pallas_call x1, Pallas kernels, levels_spread(): pl.pallas_call(window_kernel, out_shape=(shape((levels, width, rows), F32...  49.1 us
    unnamed x4, local copies, waits for them, and re-layouts  4.63 us

profile of v2, /device:TPU:29, one launch (start us, length us, event | category | flops | bytes accessed | tf_op | source)
XLA Modules:
  0.0 55.8 jit_solution(7027791446556465121)
XLA Ops:
  0.6 0.8 %fusion = (s32[64]{0:T(128)S(1)}, s32[64]{0:T(128)S(1)}) fusion(s32[128]{0:T(128)} %param.17), kind=kLoop, calls=%fused_computation.1 | loop fusion | bytes 1024 | tf_op jit(solution)/shard_map/slice | solution.py:398
  1.4 0.6 %pad_add_fusion = s32[256]{0:T(256)} fusion(s32[64]{0:T(128)S(1)} %get-tuple-element.3, s32[128]{0:T(128)S(1)} %broadcast_in_dim.3, s32[64]{0:T(128)S(1)} %get-tuple-element.2), kind=kLoop, calls=%fused_computation | loop fusion | flops 512 | bytes 2048 | tf_op jit(solution)/shard_map/concatenate | solution.py:398
  2.1 49.1 %window.1 = (f32[16,24,2048]{2,1,0:T(8,128)}, f32[24,2048]{1,0:T(8,128)}) custom-call(s32[1,1024]{1,0:T(1,128)} %bitcast.4, s32[1,1024]{1,0:T(1,128)} %bitcast.5, f32[16,1024]{1,0:T(8,128)} %kernel_hbm.1, f32[1,1024]{1,0:T(1,128)} %bitcast.6, f32[16,24,2048]{2,1,0:T(8,128)} %carry_hbm.1, bf16[16,24,2048]{2,1,0:T(8,128)(2,1)} %east_hbm.1, ...), custom_call_target="tpu_custom_call" | custom-call | tf_op jit(solution)/shard_map/window/pallas_call | solution.py:400
  51.1 0.0 copy-start
  51.2 3.9 %copy.14 = f32[16,24,2048]{2,1,0:T(8,128)} copy(f32[16,24,2048]{2,1,0:T(8,128)} %get-tuple-element.6) | data formatting | bytes 6291456
  55.1 0.0 copy-done
  55.1 0.7 %copy.15 = f32[24,2048]{1,0:T(8,128)} copy(f32[24,2048]{1,0:T(8,128)S(1)} %copy-done) | data formatting | bytes 393216
  (1 shorter events, 0.0 us)
Async XLA Ops:
  51.1 4.0 %copy-start = (f32[24,2048]{1,0:T(8,128)S(1)}, f32[24,2048]{1,0:T(8,128)}, u32[]{:S(2)}) copy-start(f32[24,2048]{1,0:T(8,128)} %get-tuple-element.7) | copy-start | bytes 589828

commit v3 on v2

--- a/solution.py
+++ b/solution.py
@@ -77,6 +77,41 @@
             return 0
 
         lax.fori_loop(1, self.lanes, one, 0)
+
+
+def lane_of(x):
+    return lax.broadcasted_iota(jnp.int32, x.shape, x.ndim - 1)
+
+
+def folded(ref):
+    rows, half = ref.shape[2], CAPS // 2
+    first = ref[:, :, :half].astype(F32)
+    last = ref[:, :, rows - half :].astype(F32)
+    polar = lane_of(first) < POLAR
+    return jnp.where(polar, first, last), jnp.where(polar, last, first)
+
+
+def unfolded(main, rest):
+    polar = lane_of(main) < POLAR
+    return jnp.concatenate([jnp.where(polar, main, rest), jnp.where(polar, rest, main)], axis=2)
+
+
+def pack(ref, main, rest):
+    width = main.shape[1]
+    ref[:, :width] = main
+    extra = rest[:, :8]
+    for g in range(1, width // 8):
+        moved = pltpu.roll(rest[:, 8 * g : 8 * g + 8], 8 * g, 2)
+        extra = jnp.where(lane_of(extra) < POLAR - 4 + 8 * g, extra, moved)
+    ref[:, width:] = extra
+
+
+def unpack(ref, width):
+    extra = ref[:, width:]
+    parts = [extra]
+    for g in range(1, width // 8):
+        parts.append(pltpu.roll(extra, CAPS // 2 - 8 * g, 2))
+    return unfolded(ref[:, :width], jnp.concatenate(parts, axis=1))
 
 
 def window_kernel(tile_hbm, cell_hbm, kernel_hbm, weight_hbm, carry_hbm, east_hbm, north_hbm,
@@ -128,10 +163,12 @@
 
     for load in loads[4:6]:
         load.wait()
-    caps[:, 0, :, :half] = east_ref[:, :, :half]
-    caps[:, 0, :, half:] = east_ref[:, :, rows - half :]
-    caps[:, 1, :, :half] = north_ref[:, :, :half]
-    caps[:, 1, :, half:] = north_ref[:, :, rows - half :]
+    east_main, east_rest = folded(east_ref)
+    north_main, north_rest = folded(north_ref)
+    caps[:, 0] = east_main.astype(BF)
+    caps[:, 1] = north_main.astype(BF)
+    rest = jnp.where(lane_of(east_rest) < POLAR + 4, east_rest, pltpu.roll(north_rest, 8, 2))
+    caps[:, 2] = rest.astype(BF)
     winds = Exchange(lanes, caps, courant, all_send.at[1], all_receive.at[1])
     winds.start()
     to_right[0] = east_ref[:, width - 2, :]
@@ -168,8 +205,7 @@
 
     scatter(0)
     scatter(rows - block)
-    ends[:, :, :half] = final_ref[:, :, :half]
-    ends[:, :, half:] = final_ref[:, :, rows - half :]
+    pack(ends, *folded(final_ref))
     polar = Exchange(lanes, ends, circles, all_send.at[2], all_receive.at[2])
     polar.start()
 
@@ -238,13 +274,16 @@
     def _():
         flux_copy(1).wait_recv()
 
+    answers = unpack(returned, width)
     lane = lax.broadcasted_iota(jnp.int32, (width, half), 1)
     lasts = []
     for i, at in enumerate((pl.ds(0, half), pl.ds(rows - half, half))):
         inside = (lane if i == 0 else half - 1 - lane) < KEEP
         side_at = pl.ds(i * half, half)
         for l in range(levels):
-            initial_ref[l, :, at] = jnp.where(inside, returned[l, :, side_at], initial_ref[l, :, at])
+            initial_ref[l, :, at] = jnp.where(
+                inside, answers[l, :, i * half : (i + 1) * half], initial_ref[l, :, at]
+            )
         flux_ref[:, at] = jnp.where(inside, flux_caps[:, side_at], flux_ref[:, at])
         lasts.append(pltpu.make_async_copy(
             initial_ref.at[:, :, at], initial_hbm.at[:, :, at], store_sem.at[levels + i]
@@ -305,15 +344,18 @@
 
 
 def polar_steps(field_ref, courant_ref, cut_ref, table_ref, wide_ref, back_ref, flux_send):
-    sources, width, lanes = field_ref.shape
+    sources, width, lanes = flux_send.shape
     nlon = sources * width
-    field = field_ref[...].reshape(nlon, lanes)
-    east = courant_ref[:, 0].astype(F32).reshape(nlon, lanes)
-    north = closed(courant_ref[:, 1].astype(F32).reshape(nlon, lanes))
+    field = unpack(field_ref, width).reshape(nlon, lanes)
+    rest = courant_ref[:, 2].astype(F32)
+    east = unfolded(courant_ref[:, 0].astype(F32), rest).reshape(nlon, lanes)
+    rest = pltpu.roll(rest, CAPS // 2 - 8, 2)
+    north = closed(unfolded(courant_ref[:, 1].astype(F32), rest).reshape(nlon, lanes))
     wave = lax.broadcasted_iota(jnp.int32, (2 * KMAX, lanes), 0)
     wave = jnp.where(wave >= KMAX, wave - KMAX, wave)
     factor = jnp.where(wave == 0, 1.0 / nlon, 2.0 / nlon)
-    scale = jnp.where(wave <= cut_ref[...], factor, 0.0)
+    cut = cut_ref[...]
+    scale = jnp.where(wave <= jnp.concatenate([cut, cut], axis=1), factor, 0.0)
     lane = lax.broadcasted_iota(jnp.int32, (nlon, lanes), 1)
     polar = (lane < POLAR) | (lane >= lanes - POLAR)
 
@@ -327,7 +369,8 @@
 
     middle = step(field)
     flux_send[...] = (field + middle).reshape(sources, width, lanes)
-    back_ref[...] = step(middle).reshape(sources, width, lanes)
+    back = step(middle).reshape(sources, width, lanes)
+    pack(back_ref, *folded(back))
 
 
 def up(x):
@@ -394,8 +437,7 @@
     slots = max(2, 4 * count // lanes)
     shape = jax.ShapeDtypeStruct
     table = full_table(nlon)
-    spare = jnp.zeros((CAPS - 2 * POLAR,), jnp.int32)
-    cut = jnp.concatenate([cutoff[:POLAR], spare, cutoff[POLAR:]]).reshape(1, CAPS)
+    cut = cutoff.reshape(1, 2 * POLAR)
     anywhere = pl.BlockSpec(memory_space=pl.ANY)
     return pl.pallas_call(
         window_kernel,
@@ -407,12 +449,12 @@
             VMEM((levels, count), F32), VMEM((1, count), F32),
             VMEM((levels, width, rows), F32),
             VMEM((levels, width, rows), BF), VMEM((levels, width, rows), BF),
-            VMEM((1, CAPS), jnp.int32),
+            VMEM((1, 2 * POLAR), jnp.int32),
             VMEM((nlon, 2 * KMAX), F32), VMEM((2 * KMAX, nlon), F32),
             VMEM((lanes, FIELDS, slots), BF), VMEM((lanes, FIELDS, slots), BF),
-            VMEM((lanes, 2, width, CAPS), BF), VMEM((lanes, 2, width, CAPS), BF),
-            VMEM((lanes, width, CAPS), F32), VMEM((lanes, width, CAPS), F32),
-            VMEM((lanes, width, CAPS), F32), VMEM((lanes, width, CAPS), F32),
+            VMEM((lanes, 3, width, CAPS // 2), BF), VMEM((lanes, 3, width, CAPS // 2), BF),
+            VMEM((lanes, width + 8, CAPS // 2), F32), VMEM((lanes, width + 8, CAPS // 2), F32),
+            VMEM((lanes, width + 8, CAPS // 2), F32), VMEM((lanes, width + 8, CAPS // 2), F32),
             VMEM((lanes, width, CAPS), F32), VMEM((width, CAPS), F32),
             VMEM((3, levels, rows), BF), VMEM((2, levels, rows), BF),
             VMEM((3, levels, rows), BF), VMEM((2, levels, rows), BF),

time: 56 us -> 46.1 us (0.82)
  the two profiles are of different devices: /device:TPU:29 before, /device:TPU:0 now
where the time goes in v3:
time: 46.1 us; the launch traced here: 45.5 us
  Pallas kernels  40.2 us (87%)
  local copies, waits for them, and re-layouts  4.63 us (10%)
  between operations  0.65 us (1%)
    pallas_call x1, Pallas kernels, levels_spread(): pl.pallas_call(window_kernel, out_shape=(shape((levels, width, rows), F32...  40.2 us
    unnamed x4, local copies, waits for them, and re-layouts  4.63 us

profile of v3, /device:TPU:0, one launch (start us, length us, event | category | flops | bytes accessed | tf_op | source)
XLA Modules:
  0.0 45.5 jit_solution(17785777206676554090)
XLA Ops:
  0.6 40.2 %window.1 = (f32[16,24,2048]{2,1,0:T(8,128)}, f32[24,2048]{1,0:T(8,128)}) custom-call(s32[1,1024]{1,0:T(1,128)} %bitcast.4, s32[1,1024]{1,0:T(1,128)} %bitcast.5, f32[16,1024]{1,0:T(8,128)} %kernel_hbm.1, f32[1,1024]{1,0:T(1,128)} %bitcast.6, f32[16,24,2048]{2,1,0:T(8,128)} %carry_hbm.1, bf16[16,24,2048]{2,1,0:T(8,128)(2,1)} %east_hbm.1, ...), custom_call_target="tpu_custom_call" | custom-call | tf_op jit(solution)/shard_map/window/pallas_call | solution.py:442
  40.9 0.0 copy-start
  40.9 3.9 %copy.14 = f32[16,24,2048]{2,1,0:T(8,128)} copy(f32[16,24,2048]{2,1,0:T(8,128)} %get-tuple-element.4) | data formatting | bytes 6291456
  44.8 0.0 copy-done
  44.8 0.7 %copy.15 = f32[24,2048]{1,0:T(8,128)} copy(f32[24,2048]{1,0:T(8,128)S(1)} %copy-done) | data formatting | bytes 393216
Async XLA Ops:
  40.9 4.0 %copy-start = (f32[24,2048]{1,0:T(8,128)S(1)}, f32[24,2048]{1,0:T(8,128)}, u32[]{:S(2)}) copy-start(f32[24,2048]{1,0:T(8,128)} %get-tuple-element.5) | copy-start | bytes 589828

commit v4 on v3

--- a/solution.py
+++ b/solution.py
@@ -13,7 +13,7 @@
 KMAX = 64
 CAPS = 256
 KEEP = 66
-FIELDS = 32
+FIELDS = 24
 
 HIGH = lax.Precision.HIGHEST
 VMEM = pltpu.VMEM
@@ -340,7 +340,7 @@
     fields = jnp.concatenate([values, extra.astype(F32)], axis=0)
     spread = [jnp.where(tile == d, fields, 0.0).astype(BF) for d in range(lanes)]
     routed = nt_dot(jnp.concatenate(spread, axis=0), place)
-    message[...] = routed.astype(BF).reshape(lanes, FIELDS, slots)
+    message[...] = routed.reshape(lanes, FIELDS, slots).astype(BF)
 
 
 def polar_steps(field_ref, courant_ref, cut_ref, table_ref, wide_ref, back_ref, flux_send):

time: 46.1 us -> 45.4 us (0.985)
  the two profiles are of different devices: /device:TPU:0 before, /device:TPU:11 now
where the time goes in v4:
time: 45.4 us; the launch traced here: 45.2 us
  Pallas kernels  39.9 us (88%)
  local copies, waits for them, and re-layouts  4.63 us (10%)
  between operations  0.65 us (1%)
    pallas_call x1, Pallas kernels, levels_spread(): pl.pallas_call(window_kernel, out_shape=(shape((levels, width, rows), F32...  39.9 us
    unnamed x4, local copies, waits for them, and re-layouts  4.63 us

profile of v4, /device:TPU:11, one launch (start us, length us, event | category | flops | bytes accessed | tf_op | source)
XLA Modules:
  0.0 45.2 jit_solution(2617956632619136461)
XLA Ops:
  0.6 39.9 %window.1 = (f32[16,24,2048]{2,1,0:T(8,128)}, f32[24,2048]{1,0:T(8,128)}) custom-call(s32[1,1024]{1,0:T(1,128)} %bitcast.4, s32[1,1024]{1,0:T(1,128)} %bitcast.5, f32[16,1024]{1,0:T(8,128)} %kernel_hbm.1, f32[1,1024]{1,0:T(1,128)} %bitcast.6, f32[16,24,2048]{2,1,0:T(8,128)} %carry_hbm.1, bf16[16,24,2048]{2,1,0:T(8,128)(2,1)} %east_hbm.1, ...), custom_call_target="tpu_custom_call" | custom-call | tf_op jit(solution)/shard_map/window/pallas_call | solution.py:442
  40.6 0.0 copy-start
  40.6 3.9 %copy.14 = f32[16,24,2048]{2,1,0:T(8,128)} copy(f32[16,24,2048]{2,1,0:T(8,128)} %get-tuple-element.4) | data formatting | bytes 6291456
  44.5 0.0 copy-done
  44.5 0.7 %copy.15 = f32[24,2048]{1,0:T(8,128)} copy(f32[24,2048]{1,0:T(8,128)S(1)} %copy-done) | data formatting | bytes 393216
Async XLA Ops:
  40.6 4.0 %copy-start = (f32[24,2048]{1,0:T(8,128)S(1)}, f32[24,2048]{1,0:T(8,128)}, u32[]{:S(2)}) copy-start(f32[24,2048]{1,0:T(8,128)} %get-tuple-element.5) | copy-start | bytes 589828
